TPU v7x, 512 devices: a whole 4x8x8 slice. The times are simulated.
512 devices in a mesh: slab: 16 (over y_lo, z), group: 32 (over x, y_hi, core).
Axes of the slice: x: 4, y: 8 (y_hi: 4, y_lo: 2; y = y_hi * 2 + y_lo), z: 8, core: 2. Of those that a mesh axis runs over, the one named last changes fastest.
Arguments:
- images: bfloat16 [131072, 768], P(('slab', 'group')), may hold values from -200 to 200
- references: bfloat16 [8192, 768], P(('slab', 'group')), may hold values from -4 to 4
- ctf_table: float32 [32, 384], replicated, may hold values from -1.3 to 1.3
- ctf_ids: int32 [131072], P(('slab', 'group')), may hold values from 0 to 31
- owners: int32 [131072], P(('slab', 'group')), may hold values from 0 to 15, as said below
Outputs:
- new_references: float32 [8192, 768], P(('slab', 'group'))
- log_evidence: float32 [131072], P(('slab', 'group'))
Inputs may be any that keep to these rules, and one draw needn't show every extreme that they name: `owners`: no slab is named by more than 48 lines of one device's 256, and in every device's lines one slab is named by exactly 48.
All inputs are finite; a program needn't handle non-finite values.
Results may differ from a plain program's by a relative error of at most 0.003.
Values may be sent and summed in bfloat16 or wider, within the bound.
A program may use at most 64 MiB of HBM per device.

v0:
```python
import jax
import jax.numpy as jnp
from jax import lax
from jax.sharding import PartitionSpec as P


def slot_plan(owner_block, slab_count, capacity):
    line_count = owner_block.shape[0]
    one_hot = (owner_block[:, None] == jnp.arange(slab_count, dtype=jnp.int32)[None, :]).astype(
        jnp.int32
    )
    earlier = jnp.cumsum(one_hot, axis=0) - one_hot
    rank_index = jnp.sum(earlier * one_hot, axis=1)
    slot_index = owner_block * capacity + rank_index
    filled_slot = (
        jnp.zeros((slab_count * capacity,), jnp.int32)
        .at[slot_index]
        .set(jnp.arange(line_count, dtype=jnp.int32) + 1)
    )
    filled_mask = filled_slot > 0
    source_row = jnp.maximum(filled_slot - 1, 0)
    return (slot_index, source_row, filled_mask)


def weigh(image_slots, ctf_tags, ctf_table):
    group_count = ctf_table.shape[0]
    levels = jnp.arange(1, group_count + 1, dtype=jnp.float32)
    group_pick = (ctf_tags.astype(jnp.float32)[:, None] == levels[None, :]).astype(jnp.float32)
    ctf_rows = jnp.dot(group_pick, ctf_table, precision=lax.Precision.HIGHEST)
    weighted = (
        image_slots.astype(jnp.float32) * jnp.concatenate([ctf_rows, ctf_rows], axis=1)
    ).astype(jnp.bfloat16)
    ctf_square = (ctf_rows * ctf_rows).astype(jnp.bfloat16)
    return (weighted, ctf_square)


def score_block(weighted, ctf_square, ref_lines):
    half_width = ref_lines.shape[1] // 2
    widened = ref_lines.astype(jnp.float32)
    line_power = (widened[:, :half_width] ** 2 + widened[:, half_width:] ** 2).astype(jnp.bfloat16)
    cross_term = lax.dot_general(
        weighted, ref_lines, (((1,), (1,)), ((), ())), preferred_element_type=jnp.float32
    )
    quad_term = lax.dot_general(
        ctf_square, line_power, (((1,), (1,)), ((), ())), preferred_element_type=jnp.float32
    )
    return (cross_term - 0.5 * quad_term) * ref_lines.shape[1] ** (-0.5)


def on_device(images, references, ctf_table, ctf_ids, owners):
    slab_count = lax.axis_size("slab")
    line_count = images.shape[0]
    capacity = 3 * line_count // slab_count
    slot_index, source_row, filled_mask = slot_plan(owners, slab_count, capacity)
    image_slots = jnp.where(filled_mask[:, None], images[source_row], jnp.zeros((), jnp.bfloat16))
    ctf_tags = jnp.where(filled_mask, ctf_ids[source_row] + 1, 0).astype(jnp.bfloat16)
    arrived_lines, arrived_tags = (
        lax.all_to_all(image_slots, "slab", split_axis=0, concat_axis=0, tiled=True),
        lax.all_to_all(ctf_tags, "slab", split_axis=0, concat_axis=0, tiled=True),
    )
    weighted, ctf_square = weigh(arrived_lines, arrived_tags, ctf_table)
    arrived_mask = arrived_tags.astype(jnp.float32) > 0.0
    scores = score_block(
        weighted, ctf_square, lax.all_gather(references, "group", axis=0, tiled=True)
    )
    score_max = jnp.max(scores, axis=1, keepdims=True)
    exp_total = jnp.sum(jnp.exp(scores - score_max), axis=1, keepdims=True)
    evidence = score_max + jnp.log(exp_total)
    responsibility = (
        jnp.exp(scores - evidence) * arrived_mask[:, None].astype(jnp.float32)
    ).astype(jnp.bfloat16)
    numerator = lax.dot_general(
        responsibility, weighted, (((0,), (0,)), ((), ())), preferred_element_type=jnp.float32
    )
    denominator = lax.dot_general(
        responsibility, ctf_square, (((0,), (0,)), ((), ())), preferred_element_type=jnp.float32
    )
    returned = lax.all_to_all(evidence[:, 0], "slab", split_axis=0, concat_axis=0, tiled=True)
    line_evidence = returned[slot_index]
    summed_num, summed_den = lax.psum((numerator, denominator), "group")
    share_rows = numerator.shape[0] // lax.axis_size("group")
    offset = lax.axis_index("group") * share_rows
    share_num = lax.dynamic_slice_in_dim(summed_num, offset, share_rows, 0)
    share_den = lax.dynamic_slice_in_dim(summed_den, offset, share_rows, 0)
    new_references = share_num / (jnp.concatenate([share_den, share_den], axis=1) + 1.0)
    return (new_references, line_evidence)


def solution(mesh):
    in_specs = (
        P(("slab", "group"), None),
        P(("slab", "group"), None),
        P(),
        P(("slab", "group")),
        P(("slab", "group")),
    )
    out_specs = (P(("slab", "group"), None), P(("slab", "group")))
    return jax.shard_map(
        on_device, mesh=mesh, in_specs=in_specs, out_specs=out_specs, check_vma=False
    )
```

profile of v0, /device:TPU:1, one launch (start us, length us, event | category | flops | bytes accessed | tf_op | source)
XLA Modules:
  0.0 413.9 jit_solution(3139050886746585395)
XLA Ops:
  7.2 0.7 fusion.14
  8.7 0.8 fusion.13
  10.2 1.4 scatter_custom_fusion
  11.6 5.0 %gather_fusion.1 = s32[768]{0:T(1024)S(1)} fusion(s32[256]{0:T(256)S(1)} %copy-done.1, s32[1024]{0:T(1024)S(1)} %pad_clamp_fusion.1), kind=kCustom, calls=%fused_computation.1 | custom fusion | bytes 9216 | tf_op jit(solution)/shard_map/gather | solution.py:56
  17.3 12.0 %all-to-all-start.1 = ((bf16[16,48,1]{1,2,0:T(2,128)(2,1)}), bf16[16,48,1]{1,2,0:T(2,128)(2,1)S(1)}, u32[]{:S(2)}, u32[]{:S(2)}) async-start(bf16[16,48,1]{1,2,0:T(2,128)(2,1)} %all_to_all.21), calls=%async_computation.1 | async-start | bytes 16384 | tf_op jit(solution)/shard_map/all_to_all | solution.py:59
  29.4 2.8 gather_fusion
  32.2 1.2 broadcast_select_fusion
  33.4 3.2 all-to-all-done.1
  36.5 4.5 %all-to-all-start = ((bf16[16,48,768]{2,1,0:T(8,128)(2,1)}), bf16[16,48,768]{2,1,0:T(8,128)(2,1)S(1)}, u32[]{:S(2)}, u32[]{:S(2)}) async-start(bf16[16,48,768]{2,1,0:T(8,128)(2,1)} %broadcast_select_fusion), calls=%async_computation | async-start | bytes 2359296 | tf_op jit(solution)/shard_map/all_to_all | solution.py:58
  41.1 56.4 %all_gather.3 = bf16[512,768]{1,0:T(8,128)(2,1)S(1)} all-gather(bf16[16,768]{1,0:T(8,128)(2,1)S(1)} %copy-done.4), channel_id=1, replica_groups=mesh['slab'=16,'group'=32] {'group'}, dimensions={0}, use_global_device_ids=true | all-gather | bytes 811008 | tf_op jit(solution)/shard_map/all_gather | solution.py:64
  97.5 1.3 convert_element_type.63
  99.4 1.6 fusion.4
  101.1 1.6 bitcast_convert_fusion
  102.7 3.1 copy.12
  105.8 2.7 fusion.18
  109.4 0.8 copy-done.2
  110.1 2.1 fusion.9
  112.2 1.5 fusion.6
  114.4 7.5 %all-to-all-start.2 = ((f32[16,48,1]{1,2,0:T(1,128)}), f32[16,48,1]{1,2,0:T(1,128)S(1)}, u32[]{:S(2)}, u32[]{:S(2)}) async-start(f32[16,48,1]{1,2,0:T(1,128)} %bitcast.4), calls=%async_computation.2 | async-start | bytes 16384 | tf_op jit(solution)/shard_map/all_to_all | solution.py:78
  122.0 7.3 %all-to-all-done.2 = f32[16,48,1]{1,2,0:T(1,128)S(1)} async-done(((f32[16,48,1]{1,2,0:T(1,128)}), f32[16,48,1]{1,2,0:T(1,128)S(1)}, u32[]{:S(2)}, u32[]{:S(2)}) %all-to-all-start.2) | async-done | bytes 3104 | tf_op jit(solution)/shard_map/all_to_all | solution.py:78
  130.6 1.9 gather_fusion.2
  132.5 272.4 %all-reduce.3.cloned.1.call-done = (f32[512,384]{1,0:T(8,128)}, f32[512,768]{1,0:T(8,128)}) async-done(((f32[512,384]{1,0:T(8,128)}, f32[512,768]{1,0:T(8,128)}), (f32[512,384]{1,0:T(8,128)}, f32[512,768]{1,0:T(8,128)})) %all-reduce.3.cloned.1.call-update) | async-done | bytes 2359312 | tf_op jit(solution)/shard_map/psum | solution.py:80
  404.9 0.7 constant_dynamic-slice_fusion
  405.6 1.4 fusion.10
  (34 shorter events, 5.8 us)
Async XLA Ops:
  7.2 22.2 %copy-start = (bf16[256,768]{1,0:T(8,128)(2,1)S(1)}, bf16[256,768]{1,0:T(8,128)(2,1)}, u32[]{:S(2)}) copy-start(bf16[256,768]{1,0:T(8,128)(2,1)} %param.5) | copy-start | bytes 1179652
  7.2 4.4 %copy-start.1 = (s32[256]{0:T(256)S(1)}, s32[256]{0:T(256)}, u32[]{:S(2)}) copy-start(s32[256]{0:T(256)} %param.8) | copy-start | bytes 3076
  17.3 19.2 %all-to-all-start.1 = ((bf16[16,48,1]{1,2,0:T(2,128)(2,1)}), bf16[16,48,1]{1,2,0:T(2,128)(2,1)S(1)}, u32[]{:S(2)}, u32[]{:S(2)}) async-start(bf16[16,48,1]{1,2,0:T(2,128)(2,1)} %all_to_all.21), calls=%async_computation.1 | async-start | bytes 16384 | tf_op jit(solution)/shard_map/all_to_all | solution.py:59
  33.4 7.8 %copy-start.4 = (bf16[16,768]{1,0:T(8,128)(2,1)S(1)}, bf16[16,768]{1,0:T(8,128)(2,1)}, u32[]{:S(2)}) copy-start(bf16[16,768]{1,0:T(8,128)(2,1)} %param.6) | copy-start | bytes 73732
  36.5 64.5 %all-to-all-start = ((bf16[16,48,768]{2,1,0:T(8,128)(2,1)}), bf16[16,48,768]{2,1,0:T(8,128)(2,1)S(1)}, u32[]{:S(2)}, u32[]{:S(2)}) async-start(bf16[16,48,768]{2,1,0:T(8,128)(2,1)} %broadcast_select_fusion), calls=%async_computation | async-start | bytes 2359296 | tf_op jit(solution)/shard_map/all_to_all | solution.py:58
  41.1 363.8 %all-reduce.3.cloned.1.call-start = ((), (), s32[]{:S(2)}) async-start(), calls=%async_computation.3 | async-start | bytes 4718592 | tf_op jit(solution)/shard_map/psum | solution.py:80
  105.8 2.7 copy-start.3
  108.5 1.7 copy-start.2
  114.4 14.9 %all-to-all-start.2 = ((f32[16,48,1]{1,2,0:T(1,128)}), f32[16,48,1]{1,2,0:T(1,128)S(1)}, u32[]{:S(2)}, u32[]{:S(2)}) async-start(f32[16,48,1]{1,2,0:T(1,128)} %bitcast.4), calls=%async_computation.2 | async-start | bytes 16384 | tf_op jit(solution)/shard_map/all_to_all | solution.py:78
Sparse Core Ops, SparseCore 0:
  113.9 290.9 all-reduce.2
where the time goes:
time: 415 us; the launch traced here: 414 us
  waiting for transfers between devices  283 us (68%)
  blocking collectives  56.4 us (14%)
  starting transfers between devices  24 us (6%)
  local copies, waits for them, and re-layouts  18 us (4%)
  between operations  14.2 us (3%)
  other arithmetic  9.84 us (2%)
  matrix products  8.53 us (2%)
    psum x1, waiting for transfers between devices, on_device(): summed_num, summed_den = lax.psum((numerator, denominator), 'group')  272 us
    all_gather x1, blocking collectives, on_device(): lax.all_gather(references, 'group', axis=0, tiled=True)  56.4 us
    all_to_all x1, starting transfers between devices, on_device(): lax.all_to_all(ctf_tags, 'slab', split_axis=0, concat_axis=0, tiled=True)  12 us
  transfers between devices with their start and end apart: 4, of which 3 were waited for; matrix products, arithmetic and copies ran while one was open for 3% of the time, Pallas kernels for 0%

commit v1 on v0

v1 whole, which is shorter than its diff:
```python
import functools

import jax
import jax.numpy as jnp
from jax import lax
from jax.experimental import pallas as pl
from jax.experimental.pallas import tpu as pltpu
from jax.sharding import PartitionSpec as P

F32, BF16 = jnp.float32, jnp.bfloat16
MESH = pl.DeviceIdType.MESH
N_YLO, N_Z = 2, 8
N_X, N_YHI, N_CORE = 4, 4, 2
OFFSETS = (
    (0, 0), (1, 0), (0, 1), (1, 1),
    (0, 7), (1, 7), (0, 2), (1, 2),
    (0, 6), (1, 6), (0, 3), (1, 3),
    (0, 5), (1, 5), (0, 4), (1, 4),
)
PER_BATCH = 4


def nt(a, b):
    return lax.dot_general(a, b, (((1,), (1,)), ((), ())), preferred_element_type=F32)


def tn(a, b):
    return lax.dot_general(a, b, (((0,), (0,)), ((), ())), preferred_element_type=F32)


def nn(a, b):
    return jnp.dot(a, b, preferred_element_type=F32)


def three(v):
    hi = v.astype(BF16)
    rest = v - hi.astype(F32)
    mid = rest.astype(BF16)
    return hi, mid, (rest - mid.astype(F32)).astype(BF16)


def iota(shape, dim):
    return lax.broadcasted_iota(jnp.int32, shape, dim)


def kernel(
    img, refs, ctf, ids, own,
    out, line_ev,
    weighted, send_lines, lines, send_tags, tags, send_ev, ev,
    ref_all, resp, quad, acc, racc, own_rows,
    core_in, rcore_out, rcore_in, x_out, x_in, rx_out, rx_in, y_out, y_in, ry_out, ry_in,
    s_line, r_line, s_tag, r_tag, s_ev, r_ev,
    s_agy, r_agy, s_agx, r_agx, s_agc, r_agc,
    s_rsc, r_rsc, s_rcc, r_rcc, s_rsx, r_rsx, s_rcx, r_rcx, s_rsy, r_rsy, s_rcy, r_rcy,
):
    rows, width = img.shape
    half = width // 2
    groups = ctf.shape[0]
    n = N_YLO * N_Z
    cap = 3 * rows // n
    batches = n // PER_BATCH
    span = PER_BATCH * cap
    slab, group = lax.axis_index("slab"), lax.axis_index("group")
    y_lo, z = slab // N_Z, slab % N_Z
    x, y_hi, core = group // (N_YHI * N_CORE), (group // N_CORE) % N_YHI, group % N_CORE

    def slab_at(dy, dz):
        return ((y_lo + dy + N_YLO) % N_YLO) * N_Z + (z + dz + N_Z) % N_Z

    def to(k):
        return (slab_at(*OFFSETS[k]), group)

    def back(k):
        return (slab_at(-OFFSETS[k][0], -OFFSETS[k][1]), group)

    def x_peer(d):
        return (slab, (((x + d) % N_X) * N_YHI + y_hi) * N_CORE + core)

    def y_peer(d):
        return (slab, (x * N_YHI + (y_hi + d) % N_YHI) * N_CORE + core)

    sibling = (slab, group + 1 - 2 * core)

    def copy(src, dst, send, recv, device):
        return pltpu.make_async_remote_copy(
            src_ref=src, dst_ref=dst, send_sem=send, recv_sem=recv, device_id=device, device_id_type=MESH
        )

    barrier = pltpu.get_barrier_semaphore()
    partners = [to(k) for k in range(1, n)]
    partners += [x_peer(d) for d in range(1, N_X)] + [y_peer(d) for d in range(1, N_YHI)] + [sibling]
    for p in partners:
        pl.semaphore_signal(barrier, inc=1, device_id=p, device_id_type=MESH)

    target = iota((n, rows), 0)
    wanted = jnp.zeros((n, rows), jnp.int32)
    for k in range(n):
        wanted = jnp.where(target == k, slab_at(*OFFSETS[k]), wanted)
    hot = (wanted == own[...]).astype(F32)
    hot_b = hot.astype(BF16)
    before = (iota((rows, rows), 0) < iota((rows, rows), 1)).astype(F32).astype(BF16)
    rank = jnp.sum(hot * nn(hot_b, before), axis=0, keepdims=True)
    line_k = jnp.sum(hot * target.astype(F32), axis=0, keepdims=True)
    slot = (line_k * cap + rank).astype(jnp.int32)
    tag_row = (ids[...] + 1).astype(F32)
    rank_hot = (iota((128, rows), 0) == rank.astype(jnp.int32)).astype(F32).astype(BF16)
    tag_slots = nt((hot * tag_row).astype(BF16), rank_hot)
    for k in range(n):
        send_tags[k] = jnp.broadcast_to(tag_slots[k : k + 1, :], (8, 128))

    pick = (iota((groups, rows), 0) == ids[...]).astype(F32).astype(BF16)
    ctf_hi, ctf_mid, ctf_lo = three(ctf[...])
    ctf_rows = tn(pick, ctf_hi) + tn(pick, ctf_mid) + tn(pick, ctf_lo)
    weighted[:, :half] = (img[:, :half].astype(F32) * ctf_rows).astype(BF16)
    weighted[:, half:] = (img[:, half:].astype(F32) * ctf_rows).astype(BF16)

    pl.semaphore_wait(barrier, len(partners))

    ref_all[core, x, y_hi] = refs[...]
    ag_y = [copy(refs, ref_all.at[core, x, y_hi], s_agy.at[d - 1], r_agy.at[d - 1], y_peer(d)) for d in range(1, N_YHI)]
    for c in ag_y:
        c.start()

    sends = []
    for b in reversed(range(batches)):
        place = (iota((span, rows), 0) + b * span == slot).astype(F32).astype(BF16)
        packed = nn(place, weighted[...]).astype(BF16)
        for j in reversed(range(PER_BATCH)):
            k = b * PER_BATCH + j
            part = packed[j * cap : (j + 1) * cap]
            if k == 0:
                lines[0] = part
                tags[0] = send_tags[0]
                continue
            send_lines[k] = part
            line_copy = copy(send_lines.at[k], lines.at[k], s_line.at[k], r_line.at[k], to(k))
            tag_copy = copy(send_tags.at[k], tags.at[k], s_tag.at[k], r_tag.at[k], to(k))
            tag_copy.start()
            line_copy.start()
            sends += [tag_copy, line_copy]

    for c in ag_y:
        c.wait_recv()
    mine = ref_all.at[core, x]
    ag_x = [copy(mine, mine, s_agx.at[d - 1], r_agx.at[d - 1], x_peer(d)) for d in range(1, N_X)]
    for c in ag_x:
        c.start()
    ag_c = []
    for d in range(N_X):
        if d:
            ag_x[d - 1].wait_recv()
        piece = ref_all.at[core, (x - d + N_X) % N_X]
        ag_c.append(copy(piece, piece, s_agc.at[d], r_agc.at[d], sibling))
        ag_c[-1].start()
    for c in ag_c:
        c.wait_recv()
    sends += ag_y + ag_x + ag_c

    k_loc = N_CORE * N_X * N_YHI * refs.shape[0]
    row_group = iota((128, half), 0)
    ctf_sq = ctf[...] * ctf[...]
    ctf_sq4 = jnp.concatenate([ctf_sq] * (128 // groups), axis=0).astype(BF16)
    del row_group
    reference = ref_all[...].reshape(k_loc, width)
    re, im = reference[:, :half].astype(F32), reference[:, half:].astype(F32)
    power = (re * re + im * im).astype(BF16)
    hi, mid, lo = three(-0.5 * nt(power, ctf_sq4))
    lane = iota((k_loc, 128), 1)
    zero = jnp.zeros((k_loc, 128), F32)
    quad[...] = jnp.where(
        lane < groups, hi.astype(F32),
        jnp.where(lane < 2 * groups, mid.astype(F32), jnp.where(lane < 3 * groups, lo.astype(F32), zero)),
    ).astype(BF16)

    scale = width**-0.5
    spread = (iota((128, span), 0) == iota((128, span), 1) % cap).astype(F32).astype(BF16)
    mine_8 = (iota((PER_BATCH * 8, span), 0) == 8 * (iota((PER_BATCH * 8, span), 1) // cap)).astype(F32)
    tag_of = (iota((128, span), 0) % groups + 1).astype(F32)
    h_rows = k_loc // N_CORE
    ev_sends, core_sends = [], []
    for b in range(batches):
        for j in range(PER_BATCH):
            k = b * PER_BATCH + j
            if k:
                copy(send_tags.at[k], tags.at[k], s_tag.at[k], r_tag.at[k], to(k)).wait_recv()
                copy(send_lines.at[k], lines.at[k], s_line.at[k], r_line.at[k], to(k)).wait_recv()
        batch = lines[b * PER_BATCH : (b + 1) * PER_BATCH].reshape(span, width)
        tag8 = tags[b * PER_BATCH : (b + 1) * PER_BATCH].reshape(PER_BATCH * 8, 128).astype(BF16)
        tag = jnp.sum(nn(tag8, spread) * mine_8, axis=0, keepdims=True)
        chosen = (tag_of == tag).astype(F32).astype(BF16)
        score = (nt(ref_all[...].reshape(k_loc, width), batch) + nn(quad[...], chosen)) * scale
        top = jnp.max(score, axis=0, keepdims=True)
        e = jnp.exp(score - top)
        total = jnp.sum(e, axis=0, keepdims=True)
        resp[...] = (e * (1.0 / total)).astype(BF16)
        evidence = top + jnp.log(total)
        send_ev[b, :, :span] = jnp.broadcast_to(evidence, (8, span))
        send_ev[b, :, span:] = jnp.zeros((8, 256 - span), F32)
        for j in range(PER_BATCH):
            k = b * PER_BATCH + j
            if k:
                ev_copy = copy(send_ev.at[b], ev.at[k], s_ev.at[k], r_ev.at[k], back(k))
                ev_copy.start()
                ev_sends.append(ev_copy)
            else:
                ev[0] = send_ev[0]
        for other in (1, 0):
            c = (core + other) % N_CORE
            r = resp[pl.ds(pl.multiple_of(c * h_rows, h_rows), h_rows), :]
            num = nn(r, batch)
            cnt = nt(r, chosen)
            if b:
                num += acc[c]
                cnt += racc[c]
            acc[c] = num
            racc[c] = cnt
            if b == batches - 1 and other:
                fold = jnp.where(iota((h_rows, 128), 1) // groups == (iota((h_rows, 128), 0) // refs.shape[0]) % N_YHI, cnt, 0.0)
                rcore_out[...] = jnp.sum(fold.reshape(N_X, N_YHI, refs.shape[0], 128), axis=1)
                rc = copy(rcore_out, rcore_in, s_rcc, r_rcc, sibling)
                rc.start()
                core_sends.append(rc)
                x_rows = h_rows // N_X
                for i, d in enumerate((2, 1, 3, 0)):
                    at = pl.ds(pl.multiple_of(((x + d) % N_X) * x_rows, x_rows), x_rows)
                    cc = copy(acc.at[c, at], core_in.at[at], s_rsc.at[i], r_rsc.at[i], sibling)
                    cc.start()
                    core_sends.append(cc)

    cnt = racc[core]
    fold = jnp.where(iota((h_rows, 128), 1) // groups == (iota((h_rows, 128), 0) // refs.shape[0]) % N_YHI, cnt, 0.0)
    fold = jnp.sum(fold.reshape(N_X, N_YHI, refs.shape[0], 128), axis=1)
    core_sends[0].wait_recv()
    rx_out[...] = fold + rcore_in[...]
    x_sends = []
    for i, d in enumerate((2, 1, 3, 0)):
        xp = (x + d) % N_X
        at = pl.ds(pl.multiple_of(xp * x_rows, x_rows), x_rows)
        core_sends[1 + i].wait_recv()
        both = acc[core, at] + core_in[at]
        if d == 0:
            own_sum = both
            continue
        x_out[d - 1] = both.astype(BF16)
        xc = copy(x_out.at[d - 1], x_in.at[d - 1], s_rsx.at[d - 1], r_rsx.at[d - 1], x_peer(d))
        rc = copy(rx_out.at[xp], rx_in.at[d - 1], s_rcx.at[d - 1], r_rcx.at[d - 1], x_peer(d))
        rc.start()
        xc.start()
        x_sends += [rc, xc]
    own_cnt = rx_out[x]
    for c in x_sends:
        c.wait_recv()
    for d in range(1, N_X):
        own_sum += x_in[d - 1].astype(F32)
        own_cnt += rx_in[d - 1]

    ry_out[...] = own_cnt
    own_rows[...] = own_sum
    y_sends = []
    for d in (2, 1, 3):
        at = pl.ds(pl.multiple_of(((y_hi + d) % N_YHI) * refs.shape[0], refs.shape[0]), refs.shape[0])
        y_out[d - 1] = own_rows[at].astype(BF16)
        yc = copy(y_out.at[d - 1], y_in.at[d - 1], s_rsy.at[d - 1], r_rsy.at[d - 1], y_peer(d))
        rc = copy(ry_out, ry_in.at[d - 1], s_rcy.at[d - 1], r_rcy.at[d - 1], y_peer(d))
        rc.start()
        yc.start()
        y_sends += [rc, yc]

    for c in ev_sends:
        c.wait_recv()
    at_lane = line_k - PER_BATCH * jnp.floor(line_k * (1.0 / PER_BATCH))
    lane_hot = (iota((256, rows), 0) == (at_lane * cap + rank).astype(jnp.int32)).astype(F32).astype(BF16)
    e_hi, e_mid, e_lo = three(ev[:, 0, :])
    by_target = nn(e_hi, lane_hot) + nn(e_mid, lane_hot) + nn(e_lo, lane_hot)
    line_ev[...] = jnp.sum(hot * by_target, axis=0, keepdims=True)

    final = own_rows[pl.ds(pl.multiple_of(y_hi * refs.shape[0], refs.shape[0]), refs.shape[0])]
    cnt = own_cnt
    for c in y_sends:
        c.wait_recv()
    for d in range(1, N_YHI):
        final += y_in[d - 1].astype(F32)
        cnt += ry_in[d - 1]
    cnt = jnp.where(iota(cnt.shape, 1) // groups == y_hi, cnt, 0.0)
    c_hi, c_mid, c_lo = three(cnt)
    den = nn(c_hi, ctf_sq4) + nn(c_mid, ctf_sq4) + nn(c_lo, ctf_sq4) + 1.0
    out[:, :half] = final[:, :half] / den
    out[:, half:] = final[:, half:] / den

    for c in sends + ev_sends + core_sends + x_sends + y_sends:
        c.wait_send()


def on_device(images, references, ctf_table, ctf_ids, owners):
    rows, width = images.shape
    per = references.shape[0]
    n = N_YLO * N_Z
    cap = 3 * rows // n
    h_rows = N_X * N_YHI * per
    x_rows = N_YHI * per
    dma = pltpu.SemaphoreType.DMA
    vm = pltpu.VMEM
    scratch = [
        vm((rows, width), BF16), vm((n, cap, width), BF16), vm((n, cap, width), BF16),
        vm((n, 8, 128), F32), vm((n, 8, 128), F32), vm((n // PER_BATCH, 8, 256), F32), vm((n, 8, 256), F32),
        vm((N_CORE, N_X, N_YHI, per, width), BF16), vm((N_CORE * h_rows, PER_BATCH * cap), BF16),
        vm((N_CORE * h_rows, 128), BF16), vm((N_CORE, h_rows, width), F32), vm((N_CORE, h_rows, 128), F32), vm((x_rows, width), F32),
        vm((h_rows, width), F32), vm((N_X, per, 128), F32), vm((N_X, per, 128), F32),
        vm((N_X - 1, x_rows, width), BF16), vm((N_X - 1, x_rows, width), BF16),
        vm((N_X, per, 128), F32), vm((N_X - 1, per, 128), F32),
        vm((N_YHI - 1, per, width), BF16), vm((N_YHI - 1, per, width), BF16),
        vm((per, 128), F32), vm((N_YHI - 1, per, 128), F32),
        *[dma((n,))] * 6,
        *[dma((N_YHI - 1,))] * 2, *[dma((N_X - 1,))] * 2, *[dma((N_X,))] * 2,
        *[dma((N_X,))] * 2, dma, dma, *[dma((N_X - 1,))] * 4, *[dma((N_YHI - 1,))] * 4,
    ]
    new, ev = pl.pallas_call(
        kernel,
        out_shape=(jax.ShapeDtypeStruct((per, width), F32), jax.ShapeDtypeStruct((1, rows), F32)),
        in_specs=[pl.BlockSpec(memory_space=pltpu.VMEM)] * 5,
        out_specs=[pl.BlockSpec(memory_space=pltpu.VMEM)] * 2,
        scratch_shapes=scratch,
        compiler_params=pltpu.CompilerParams(
            collective_id=0, has_side_effects=True, vmem_limit_bytes=48 * 2**20
        ),
    )(images, references, ctf_table, ctf_ids.reshape(1, rows), owners.reshape(1, rows))
    return new, ev.reshape(rows)


def solution(mesh):
    both = P(("slab", "group"))
    rows = P(("slab", "group"), None)
    return jax.shard_map(
        on_device, mesh=mesh, in_specs=(rows, rows, P(), both, both), out_specs=(rows, both), check_vma=False
    )
```

time: 415 us -> 73.4 us (0.18)
  waiting for transfers between devices: 283 us -> 0 us
  Pallas kernels: 0 us -> 68.1 us
  blocking collectives: 56.4 us -> 0 us
  starting transfers between devices: 24 us -> 0 us
  local copies, waits for them, and re-layouts: 18 us -> 4.39 us
  between operations: 14.2 us -> 0.66 us
  other arithmetic: 9.84 us -> 0 us
  matrix products: 8.53 us -> 0 us
    psum x1 -> x0, waiting for transfers between devices: 272 us -> none  [on_device(): summed_num, summed_den = lax.psum((numerator, denominator), 'group')]
    pallas_call x0 -> x1, Pallas kernels: none -> 68.1 us  [on_device(): pl.pallas_call(kernel, out_shape=(jax.ShapeDtypeStruct((per, width), F32)...]
    all_gather x1 -> x0, blocking collectives: 56.4 us -> none  [on_device(): lax.all_gather(references, 'group', axis=0, tiled=True)]
    all_to_all x3 -> x0, starting transfers between devices: 24 us -> none  [the longest x1 12 us: on_device(): lax.all_to_all(ctf_tags, 'slab', split_axis=0, concat_axis=0, tiled=True)]
    all_to_all x3 -> x0, waiting for transfers between devices: 10.5 us -> none  [the longest x1 7.35 us: on_device(): lax.all_to_all(evidence[:, 0], 'slab', split_axis=0, concat_axis=0, tiled...]
    gather x3 -> x0, local copies, waits for them, and re-layouts: 9.67 us -> none  [the longest x1 4.98 us: on_device(): ctf_ids[source_row] + 1]
    dot_general x5 -> x0, matrix products: 8.53 us -> none  [the longest x1 2.68 us: score_block(): lax.dot_general(weighted, ref_lines, (((1,), (1,)), ((), ())), preferred_...]
  transfers between devices with their start and end apart: 4 -> 0, of which waited for: 3 -> 0; matrix products, arithmetic and copies ran while one was open for 3% -> 0% of each run, Pallas kernels for 0% -> 0%
where the time goes in v1:
time: 73.4 us; the launch traced here: 73.1 us
  Pallas kernels  68.1 us (93%)
  local copies, waits for them, and re-layouts  4.39 us (6%)
    pallas_call x1, Pallas kernels, on_device(): pl.pallas_call(kernel, out_shape=(jax.ShapeDtypeStruct((per, width), F32)...  68.1 us
    unnamed x12, local copies, waits for them, and re-layouts  4.39 us

profile of v1, /device:TPU:1, one launch (start us, length us, event | category | flops | bytes accessed | tf_op | source)
XLA Modules:
  0.0 73.1 jit_solution(13844517826250166575)
XLA Ops:
  0.6 0.0 copy-start.4
  0.6 0.0 copy-start.3
  0.7 0.7 copy-done.4
  1.3 0.0 copy-done.3
  1.3 0.0 copy-start
  1.3 1.0 %copy-done = bf16[256,768]{1,0:T(8,128)(2,1)S(1)} copy-done((bf16[256,768]{1,0:T(8,128)(2,1)S(1)}, bf16[256,768]{1,0:T(8,128)(2,1)}, u32[]{:S(2)}) %copy-start) | copy-done | bytes 393240
  2.3 0.0 copy-start.1
  2.3 0.8 %copy-done.1 = f32[32,384]{1,0:T(8,128)S(1)} copy-done((f32[32,384]{1,0:T(8,128)S(1)}, f32[32,384]{1,0:T(8,128)}, u32[]{:S(2)}) %copy-start.1) | copy-done | bytes 49176
  3.1 0.0 copy-start.2
  3.1 0.7 %copy-done.2 = bf16[16,768]{1,0:T(8,128)(2,1)S(1)} copy-done((bf16[16,768]{1,0:T(8,128)(2,1)S(1)}, bf16[16,768]{1,0:T(8,128)(2,1)}, u32[]{:S(2)}) %copy-start.2) | copy-done | bytes 24600
  3.9 68.1 %shard_map.68 = (f32[16,768]{1,0:T(8,128)S(1)}, f32[1,256]{1,0:T(1,128)S(1)}) custom-call(bf16[256,768]{1,0:T(8,128)(2,1)S(1)} %copy-done, bf16[16,768]{1,0:T(8,128)(2,1)S(1)} %copy-done.2, f32[32,384]{1,0:T(8,128)S(1)} %copy-done.1, s32[1,256]{1,0:T(1,128)S(1)} %bitcast.3, s32[1,256]{1,0:T(1,128)S(1)} %bitcast.4), custom_call_target="tpu_custom_call" | custom-call | tf_op jit(solution)/shard_map/pallas_call | solution.py:317
  71.9 0.6 copy.9
  72.6 0.6 copy.10
Async XLA Ops:
  0.6 0.7 copy-start.4
  0.6 0.7 copy-start.3
  1.3 1.0 %copy-start = (bf16[256,768]{1,0:T(8,128)(2,1)S(1)}, bf16[256,768]{1,0:T(8,128)(2,1)}, u32[]{:S(2)}) copy-start(bf16[256,768]{1,0:T(8,128)(2,1)} %img.1) | copy-start | bytes 1179652
  2.3 0.8 %copy-start.1 = (f32[32,384]{1,0:T(8,128)S(1)}, f32[32,384]{1,0:T(8,128)}, u32[]{:S(2)}) copy-start(f32[32,384]{1,0:T(8,128)} %ctf.1) | copy-start | bytes 147460
  3.1 0.7 %copy-start.2 = (bf16[16,768]{1,0:T(8,128)(2,1)S(1)}, bf16[16,768]{1,0:T(8,128)(2,1)}, u32[]{:S(2)}) copy-start(bf16[16,768]{1,0:T(8,128)(2,1)} %refs.1) | copy-start | bytes 73732

commit v2 on v1

--- a/solution.py
+++ b/solution.py
@@ -9,14 +9,10 @@
 
 F32, BF16 = jnp.float32, jnp.bfloat16
 MESH = pl.DeviceIdType.MESH
-N_YLO, N_Z = 2, 8
-N_X, N_YHI, N_CORE = 4, 4, 2
-OFFSETS = (
-    (0, 0), (1, 0), (0, 1), (1, 1),
-    (0, 7), (1, 7), (0, 2), (1, 2),
-    (0, 6), (1, 6), (0, 3), (1, 3),
-    (0, 5), (1, 5), (0, 4), (1, 4),
-)
+N_X, N_Y, N_Z = 4, 8, 8
+N_YLO, N_YHI, N_CORE = 2, 4, 2
+FAR = N_Z // 2
+OFFSETS = tuple((dz, dx * (1 - 2 * dy), dy) for dz in (0, 1, -1, 2) for dy in (0, 1) for dx in (0, 1))
 PER_BATCH = 4
 
 
@@ -47,39 +43,52 @@
     img, refs, ctf, ids, own,
     out, line_ev,
     weighted, send_lines, lines, send_tags, tags, send_ev, ev,
-    ref_all, resp, quad, acc, racc, own_rows,
-    core_in, rcore_out, rcore_in, x_out, x_in, rx_out, rx_in, y_out, y_in, ry_out, ry_in,
+    ref_all, resp, quad, acc, racc,
+    core_in, rcore_out, rcore_in, x_out, x_in, rx_out, rx_in, own_rows, y_out, y_in, ry_out, ry_in,
+    fin_out, fin_in,
     s_line, r_line, s_tag, r_tag, s_ev, r_ev,
-    s_agy, r_agy, s_agx, r_agx, s_agc, r_agc,
+    s_ag, r_ag, s_agy, r_agy, s_agx, r_agx, s_agc, r_agc,
     s_rsc, r_rsc, s_rcc, r_rcc, s_rsx, r_rsx, s_rcx, r_rcx, s_rsy, r_rsy, s_rcy, r_rcy,
+    s_fin, r_fin,
 ):
     rows, width = img.shape
+    per = refs.shape[0]
     half = width // 2
     groups = ctf.shape[0]
-    n = N_YLO * N_Z
+    n = len(OFFSETS)
     cap = 3 * rows // n
     batches = n // PER_BATCH
     span = PER_BATCH * cap
     slab, group = lax.axis_index("slab"), lax.axis_index("group")
     y_lo, z = slab // N_Z, slab % N_Z
     x, y_hi, core = group // (N_YHI * N_CORE), (group // N_CORE) % N_YHI, group % N_CORE
-
-    def slab_at(dy, dz):
-        return ((y_lo + dy + N_YLO) % N_YLO) * N_Z + (z + dz + N_Z) % N_Z
+    y = N_YLO * y_hi + y_lo
+    way = 1 - 2 * core
+    odd, pair = x % 2, x // 2
+
+    def device(dz, dx, dy):
+        x_to, y_to, z_to = (x + dx + N_X) % N_X, (y + dy + N_Y) % N_Y, (z + dz + N_Z) % N_Z
+        return (y_to % N_YLO) * N_Z + z_to, (x_to * N_YHI + y_to // N_YLO) * N_CORE + core
 
     def to(k):
-        return (slab_at(*OFFSETS[k]), group)
+        return device(*(way * d for d in OFFSETS[k]))
 
     def back(k):
-        return (slab_at(-OFFSETS[k][0], -OFFSETS[k][1]), group)
-
-    def x_peer(d):
-        return (slab, (((x + d) % N_X) * N_YHI + y_hi) * N_CORE + core)
+        return device(*(-way * d for d in OFFSETS[k]))
+
+    def slab_of(k):
+        dz, dx, dy = (way * d for d in OFFSETS[k])
+        return ((y + dy + N_Y) % N_YLO) * N_Z + (z + dz + N_Z + FAR * ((x + dx + N_X) % 2)) % N_Z
 
     def y_peer(d):
-        return (slab, (x * N_YHI + (y_hi + d) % N_YHI) * N_CORE + core)
-
-    sibling = (slab, group + 1 - 2 * core)
+        return device(0, 0, N_YLO * d)
+
+    x_peer = device(0, 2, 0)
+    sibling = (slab, group + way)
+    near, across, beyond = device(0, 1 - 2 * odd, 0), device(FAR, 1 - 2 * odd, 0), device(FAR, 0, 0)
+
+    def choose(a, b):
+        return tuple(odd * v + (1 - odd) * u for u, v in zip(a, b))
 
     def copy(src, dst, send, recv, device):
         return pltpu.make_async_remote_copy(
@@ -87,15 +96,19 @@
         )
 
     barrier = pltpu.get_barrier_semaphore()
-    partners = [to(k) for k in range(1, n)]
-    partners += [x_peer(d) for d in range(1, N_X)] + [y_peer(d) for d in range(1, N_YHI)] + [sibling]
+    partners = [to(k) for k in range(1, n)] + [back(k) for k in range(1, n)]
+    partners += [y_peer(d) for d in range(1, N_YHI)] + [x_peer, sibling, near, across]
     for p in partners:
         pl.semaphore_signal(barrier, inc=1, device_id=p, device_id_type=MESH)
+
+    @pl.when(odd == 1)
+    def _():
+        pl.semaphore_signal(barrier, inc=1, device_id=beyond, device_id_type=MESH)
 
     target = iota((n, rows), 0)
     wanted = jnp.zeros((n, rows), jnp.int32)
     for k in range(n):
-        wanted = jnp.where(target == k, slab_at(*OFFSETS[k]), wanted)
+        wanted = jnp.where(target == k, slab_of(k), wanted)
     hot = (wanted == own[...]).astype(F32)
     hot_b = hot.astype(BF16)
     before = (iota((rows, rows), 0) < iota((rows, rows), 1)).astype(F32).astype(BF16)
@@ -114,12 +127,20 @@
     weighted[:, :half] = (img[:, :half].astype(F32) * ctf_rows).astype(BF16)
     weighted[:, half:] = (img[:, half:].astype(F32) * ctf_rows).astype(BF16)
 
-    pl.semaphore_wait(barrier, len(partners))
-
-    ref_all[core, x, y_hi] = refs[...]
-    ag_y = [copy(refs, ref_all.at[core, x, y_hi], s_agy.at[d - 1], r_agy.at[d - 1], y_peer(d)) for d in range(1, N_YHI)]
-    for c in ag_y:
-        c.start()
+    pl.semaphore_wait(barrier, len(partners) + odd)
+
+    slot_ref = ref_all.at[core, pair, y_hi, odd]
+    ag = copy(refs, slot_ref, s_ag.at[0], r_ag.at[odd], choose(across, near))
+    ag.start()
+    ag_2 = copy(refs, slot_ref, s_ag.at[1], r_ag.at[1], beyond)
+
+    @pl.when(odd == 1)
+    def _():
+        ag_2.start()
+
+    @pl.when(odd == 0)
+    def _():
+        ref_all[core, pair, y_hi, 0] = refs[...]
 
     sends = []
     for b in reversed(range(batches)):
@@ -139,28 +160,32 @@
             line_copy.start()
             sends += [tag_copy, line_copy]
 
+    @pl.when(odd == 1)
+    def _():
+        copy(refs, ref_all.at[core, pair, y_hi, 0], s_ag.at[0], r_ag.at[0], across).wait_recv()
+        ag_2.wait_send()
+
+    copy(refs, ref_all.at[core, pair, y_hi, 1], s_ag.at[0], r_ag.at[1], across).wait_recv()
+    mine = ref_all.at[core, pair, y_hi]
+    ag_y = [copy(mine, mine, s_agy.at[d - 1], r_agy.at[d - 1], y_peer(d)) for d in range(1, N_YHI)]
     for c in ag_y:
-        c.wait_recv()
-    mine = ref_all.at[core, x]
-    ag_x = [copy(mine, mine, s_agx.at[d - 1], r_agx.at[d - 1], x_peer(d)) for d in range(1, N_X)]
-    for c in ag_x:
         c.start()
-    ag_c = []
-    for d in range(N_X):
-        if d:
-            ag_x[d - 1].wait_recv()
-        piece = ref_all.at[core, (x - d + N_X) % N_X]
-        ag_c.append(copy(piece, piece, s_agc.at[d], r_agc.at[d], sibling))
-        ag_c[-1].start()
+    for c in ag_y:
+        c.wait_recv()
+    mine, theirs = ref_all.at[core, pair], ref_all.at[core, 1 - pair]
+    ag_x = [copy(mine, mine, s_agx, r_agx, x_peer)]
+    ag_x[0].start()
+    ag_c = [copy(p, p, s_agc.at[i], r_agc.at[i], sibling) for i, p in enumerate((mine, theirs))]
+    ag_c[0].start()
+    ag_x[0].wait_recv()
+    ag_c[1].start()
     for c in ag_c:
         c.wait_recv()
-    sends += ag_y + ag_x + ag_c
-
-    k_loc = N_CORE * N_X * N_YHI * refs.shape[0]
-    row_group = iota((128, half), 0)
+    sends += [ag] + ag_y + ag_x + ag_c
+
+    k_loc = N_CORE * N_X * N_YHI * per
     ctf_sq = ctf[...] * ctf[...]
     ctf_sq4 = jnp.concatenate([ctf_sq] * (128 // groups), axis=0).astype(BF16)
-    del row_group
     reference = ref_all[...].reshape(k_loc, width)
     re, im = reference[:, :half].astype(F32), reference[:, half:].astype(F32)
     power = (re * re + im * im).astype(BF16)
@@ -214,52 +239,47 @@
                 cnt += racc[c]
             acc[c] = num
             racc[c] = cnt
+            if b == batches - 1:
+                own_lanes = iota((h_rows, 128), 1) // groups == (iota((h_rows, 128), 0) // (2 * per)) % N_YHI
+                fold = jnp.where(own_lanes, cnt, 0.0).reshape(2, N_YHI, 2 * per, 128)
+                fold = jnp.sum(fold, axis=1)
             if b == batches - 1 and other:
-                fold = jnp.where(iota((h_rows, 128), 1) // groups == (iota((h_rows, 128), 0) // refs.shape[0]) % N_YHI, cnt, 0.0)
-                rcore_out[...] = jnp.sum(fold.reshape(N_X, N_YHI, refs.shape[0], 128), axis=1)
+                rcore_out[...] = fold
                 rc = copy(rcore_out, rcore_in, s_rcc, r_rcc, sibling)
                 rc.start()
                 core_sends.append(rc)
-                x_rows = h_rows // N_X
-                for i, d in enumerate((2, 1, 3, 0)):
-                    at = pl.ds(pl.multiple_of(((x + d) % N_X) * x_rows, x_rows), x_rows)
+                x_rows = h_rows // 2
+                for i, xp in enumerate((1 - pair, pair)):
+                    at = pl.ds(pl.multiple_of(xp * x_rows, x_rows), x_rows)
                     cc = copy(acc.at[c, at], core_in.at[at], s_rsc.at[i], r_rsc.at[i], sibling)
                     cc.start()
                     core_sends.append(cc)
 
-    cnt = racc[core]
-    fold = jnp.where(iota((h_rows, 128), 1) // groups == (iota((h_rows, 128), 0) // refs.shape[0]) % N_YHI, cnt, 0.0)
-    fold = jnp.sum(fold.reshape(N_X, N_YHI, refs.shape[0], 128), axis=1)
     core_sends[0].wait_recv()
     rx_out[...] = fold + rcore_in[...]
     x_sends = []
-    for i, d in enumerate((2, 1, 3, 0)):
-        xp = (x + d) % N_X
+    for i, xp in enumerate((1 - pair, pair)):
         at = pl.ds(pl.multiple_of(xp * x_rows, x_rows), x_rows)
         core_sends[1 + i].wait_recv()
         both = acc[core, at] + core_in[at]
-        if d == 0:
-            own_sum = both
+        if i:
+            own_rows[...] = both
             continue
-        x_out[d - 1] = both.astype(BF16)
-        xc = copy(x_out.at[d - 1], x_in.at[d - 1], s_rsx.at[d - 1], r_rsx.at[d - 1], x_peer(d))
-        rc = copy(rx_out.at[xp], rx_in.at[d - 1], s_rcx.at[d - 1], r_rcx.at[d - 1], x_peer(d))
+        x_out[...] = both.astype(BF16)
+        xc = copy(x_out, x_in, s_rsx, r_rsx, x_peer)
+        rc = copy(rx_out.at[xp], rx_in, s_rcx, r_rcx, x_peer)
         rc.start()
         xc.start()
         x_sends += [rc, xc]
-    own_cnt = rx_out[x]
     for c in x_sends:
         c.wait_recv()
-    for d in range(1, N_X):
-        own_sum += x_in[d - 1].astype(F32)
-        own_cnt += rx_in[d - 1]
+    own_cnt = rx_out[pair] + rx_in[...]
 
     ry_out[...] = own_cnt
-    own_rows[...] = own_sum
     y_sends = []
     for d in (2, 1, 3):
-        at = pl.ds(pl.multiple_of(((y_hi + d) % N_YHI) * refs.shape[0], refs.shape[0]), refs.shape[0])
-        y_out[d - 1] = own_rows[at].astype(BF16)
+        at = pl.ds(pl.multiple_of(((y_hi + d) % N_YHI) * 2 * per, 2 * per), 2 * per)
+        y_out[d - 1] = (own_rows[at] + x_in[at].astype(F32)).astype(BF16)
         yc = copy(y_out.at[d - 1], y_in.at[d - 1], s_rsy.at[d - 1], r_rsy.at[d - 1], y_peer(d))
         rc = copy(ry_out, ry_in.at[d - 1], s_rcy.at[d - 1], r_rcy.at[d - 1], y_peer(d))
         rc.start()
@@ -274,45 +294,69 @@
     by_target = nn(e_hi, lane_hot) + nn(e_mid, lane_hot) + nn(e_lo, lane_hot)
     line_ev[...] = jnp.sum(hot * by_target, axis=0, keepdims=True)
 
-    final = own_rows[pl.ds(pl.multiple_of(y_hi * refs.shape[0], refs.shape[0]), refs.shape[0])]
-    cnt = own_cnt
+    at = pl.ds(pl.multiple_of(y_hi * 2 * per, 2 * per), 2 * per)
+    part = own_rows[at] + x_in[at].astype(F32)
     for c in y_sends:
         c.wait_recv()
     for d in range(1, N_YHI):
-        final += y_in[d - 1].astype(F32)
-        cnt += ry_in[d - 1]
+        part += y_in[d - 1].astype(F32)
+        own_cnt += ry_in[d - 1]
+    fin_out[:, :, :width] = part.reshape(2, per, width)
+    fin_out[:, :, width:] = own_cnt.reshape(2, per, 128)
+    fin = copy(fin_out.at[1 - odd], fin_in.at[odd], s_fin.at[0], r_fin.at[odd], choose(near, across))
+    fin.start()
+    fin_2 = copy(fin_out.at[1], fin_in.at[1], s_fin.at[1], r_fin.at[1], beyond)
+
+    @pl.when(odd == 1)
+    def _():
+        fin_2.start()
+        copy(fin_out.at[0], fin_in.at[0], s_fin.at[0], r_fin.at[0], near).wait_recv()
+
+    @pl.when(odd == 0)
+    def _():
+        fin_in[0] = fin_out[0]
+
+    copy(fin_out.at[0], fin_in.at[1], s_fin.at[0], r_fin.at[1], near).wait_recv()
+    final = fin_in[0] + fin_in[1]
+    cnt = final[:, width:]
     cnt = jnp.where(iota(cnt.shape, 1) // groups == y_hi, cnt, 0.0)
     c_hi, c_mid, c_lo = three(cnt)
     den = nn(c_hi, ctf_sq4) + nn(c_mid, ctf_sq4) + nn(c_lo, ctf_sq4) + 1.0
     out[:, :half] = final[:, :half] / den
-    out[:, half:] = final[:, half:] / den
-
-    for c in sends + ev_sends + core_sends + x_sends + y_sends:
+    out[:, half:] = final[:, half:width] / den
+
+    @pl.when(odd == 1)
+    def _():
+        fin_2.wait_send()
+
+    for c in sends + ev_sends + core_sends + x_sends + y_sends + [fin]:
         c.wait_send()
 
 
 def on_device(images, references, ctf_table, ctf_ids, owners):
     rows, width = images.shape
     per = references.shape[0]
-    n = N_YLO * N_Z
+    n = len(OFFSETS)
     cap = 3 * rows // n
     h_rows = N_X * N_YHI * per
-    x_rows = N_YHI * per
+    x_rows = h_rows // 2
     dma = pltpu.SemaphoreType.DMA
     vm = pltpu.VMEM
     scratch = [
         vm((rows, width), BF16), vm((n, cap, width), BF16), vm((n, cap, width), BF16),
         vm((n, 8, 128), F32), vm((n, 8, 128), F32), vm((n // PER_BATCH, 8, 256), F32), vm((n, 8, 256), F32),
-        vm((N_CORE, N_X, N_YHI, per, width), BF16), vm((N_CORE * h_rows, PER_BATCH * cap), BF16),
-        vm((N_CORE * h_rows, 128), BF16), vm((N_CORE, h_rows, width), F32), vm((N_CORE, h_rows, 128), F32), vm((x_rows, width), F32),
-        vm((h_rows, width), F32), vm((N_X, per, 128), F32), vm((N_X, per, 128), F32),
-        vm((N_X - 1, x_rows, width), BF16), vm((N_X - 1, x_rows, width), BF16),
-        vm((N_X, per, 128), F32), vm((N_X - 1, per, 128), F32),
-        vm((N_YHI - 1, per, width), BF16), vm((N_YHI - 1, per, width), BF16),
-        vm((per, 128), F32), vm((N_YHI - 1, per, 128), F32),
+        vm((N_CORE, 2, N_YHI, 2, per, width), BF16), vm((N_CORE * h_rows, PER_BATCH * cap), BF16),
+        vm((N_CORE * h_rows, 128), BF16), vm((N_CORE, h_rows, width), F32), vm((N_CORE, h_rows, 128), F32),
+        vm((h_rows, width), F32), vm((2, 2 * per, 128), F32), vm((2, 2 * per, 128), F32),
+        vm((x_rows, width), BF16), vm((x_rows, width), BF16), vm((2, 2 * per, 128), F32), vm((2 * per, 128), F32),
+        vm((x_rows, width), F32),
+        vm((N_YHI - 1, 2 * per, width), BF16), vm((N_YHI - 1, 2 * per, width), BF16),
+        vm((2 * per, 128), F32), vm((N_YHI - 1, 2 * per, 128), F32),
+        vm((2, per, width + 128), F32), vm((2, per, width + 128), F32),
         *[dma((n,))] * 6,
-        *[dma((N_YHI - 1,))] * 2, *[dma((N_X - 1,))] * 2, *[dma((N_X,))] * 2,
-        *[dma((N_X,))] * 2, dma, dma, *[dma((N_X - 1,))] * 4, *[dma((N_YHI - 1,))] * 4,
+        *[dma((2,))] * 2, *[dma((N_YHI - 1,))] * 2, *[dma] * 2, *[dma((2,))] * 2,
+        *[dma((2,))] * 2, *[dma] * 6, *[dma((N_YHI - 1,))] * 4,
+        *[dma((2,))] * 2,
     ]
     new, ev = pl.pallas_call(
         kernel,

time: 73.4 us -> 75 us (1.022)
  the two profiles are of different devices: /device:TPU:1 before, /device:TPU:2 now
where the time goes in v2:
time: 75 us; the launch traced here: 74.7 us
  Pallas kernels  69.6 us (93%)
  local copies, waits for them, and re-layouts  4.39 us (6%)
    pallas_call x1, Pallas kernels, on_device(): pl.pallas_call(kernel, out_shape=(jax.ShapeDtypeStruct((per, width), F32)...  69.6 us
    unnamed x12, local copies, waits for them, and re-layouts  4.39 us

profile of v2, /device:TPU:2, one launch (start us, length us, event | category | flops | bytes accessed | tf_op | source)
XLA Modules:
  0.0 74.7 jit_solution(1785458701885069057)
XLA Ops:
  0.6 0.0 copy-start.4
  0.6 0.0 copy-start.3
  0.7 0.7 copy-done.4
  1.3 0.0 copy-done.3
  1.3 0.0 copy-start
  1.3 1.0 %copy-done = bf16[256,768]{1,0:T(8,128)(2,1)S(1)} copy-done((bf16[256,768]{1,0:T(8,128)(2,1)S(1)}, bf16[256,768]{1,0:T(8,128)(2,1)}, u32[]{:S(2)}) %copy-start) | copy-done | bytes 393240
  2.3 0.0 copy-start.1
  2.3 0.8 %copy-done.1 = f32[32,384]{1,0:T(8,128)S(1)} copy-done((f32[32,384]{1,0:T(8,128)S(1)}, f32[32,384]{1,0:T(8,128)}, u32[]{:S(2)}) %copy-start.1) | copy-done | bytes 49176
  3.1 0.0 copy-start.2
  3.1 0.7 copy-done.2
  3.9 69.6 %shard_map.68 = (f32[16,768]{1,0:T(8,128)S(1)}, f32[1,256]{1,0:T(1,128)S(1)}) custom-call(bf16[256,768]{1,0:T(8,128)(2,1)S(1)} %copy-done, bf16[16,768]{1,0:T(8,128)(2,1)S(1)} %copy-done.2, f32[32,384]{1,0:T(8,128)S(1)} %copy-done.1, s32[1,256]{1,0:T(1,128)S(1)} %bitcast.3, s32[1,256]{1,0:T(1,128)S(1)} %bitcast.4), custom_call_target="tpu_custom_call" | custom-call | tf_op jit(solution)/shard_map/pallas_call | solution.py:361
  73.5 0.6 copy.9
  74.1 0.6 copy.10
Async XLA Ops:
  0.6 0.7 copy-start.4
  0.6 0.7 copy-start.3
  1.3 1.0 %copy-start = (bf16[256,768]{1,0:T(8,128)(2,1)S(1)}, bf16[256,768]{1,0:T(8,128)(2,1)}, u32[]{:S(2)}) copy-start(bf16[256,768]{1,0:T(8,128)(2,1)} %img.1) | copy-start | bytes 1179652
  2.3 0.8 %copy-start.1 = (f32[32,384]{1,0:T(8,128)S(1)}, f32[32,384]{1,0:T(8,128)}, u32[]{:S(2)}) copy-start(f32[32,384]{1,0:T(8,128)} %ctf.1) | copy-start | bytes 147460
  3.1 0.7 copy-start.2

commit v3 on v2

v3 whole, which is shorter than its diff:
```python
import functools

import jax
import jax.numpy as jnp
from jax import lax
from jax.experimental import pallas as pl
from jax.experimental.pallas import tpu as pltpu
from jax.sharding import PartitionSpec as P

F32, BF16 = jnp.float32, jnp.bfloat16
MESH = pl.DeviceIdType.MESH
N_X, N_Y, N_Z = 4, 8, 8
N_YLO, N_YHI, N_CORE = 2, 4, 2
FAR = N_Z // 2
OFFSETS = tuple((dz, dx * (1 - 2 * dy), dy) for dz in (0, 1, -1, 2) for dy in (0, 1) for dx in (0, 1))
PER_BATCH = 8


def nt(a, b):
    return lax.dot_general(a, b, (((1,), (1,)), ((), ())), preferred_element_type=F32)


def tn(a, b):
    return lax.dot_general(a, b, (((0,), (0,)), ((), ())), preferred_element_type=F32)


def nn(a, b):
    return jnp.dot(a, b, preferred_element_type=F32)


def three(v):
    hi = v.astype(BF16)
    rest = v - hi.astype(F32)
    mid = rest.astype(BF16)
    return hi, mid, (rest - mid.astype(F32)).astype(BF16)


def iota(shape, dim):
    return lax.broadcasted_iota(jnp.int32, shape, dim)


def kernel(
    img_hbm, refs_hbm, ctf_hbm, ids_hbm, own_hbm,
    out, line_ev,
    img, refs, ctf, ids, own,
    weighted, send_lines, lines, send_tags, tags, send_ev, ev,
    ref_all, resp, chosen, quad, acc, racc,
    core_in, rcore_out, rcore_in, x_out, x_in, rx_out, rx_in, own_rows, y_out, y_in, ry_out, ry_in,
    fin_out, fin_in, rfin_out, rfin_in,
    s_in,
    s_line, r_line, s_tag, r_tag, s_ev, r_ev,
    s_ag, r_ag, s_agy, r_agy, s_agx, r_agx, s_agc, r_agc,
    s_rsc, r_rsc, s_rcc, r_rcc, s_rsx, r_rsx, s_rcx, r_rcx, s_rsy, r_rsy, s_rcy, r_rcy,
    s_fin, r_fin, s_rfin, r_rfin,
):
    rows, width = img.shape
    per = refs.shape[0]
    half = width // 2
    groups = ctf.shape[0]
    n = len(OFFSETS)
    cap = 3 * rows // n
    batches = n // PER_BATCH
    span = PER_BATCH * cap
    slab, group = lax.axis_index("slab"), lax.axis_index("group")
    y_lo, z = slab // N_Z, slab % N_Z
    x, y_hi, core = group // (N_YHI * N_CORE), (group // N_CORE) % N_YHI, group % N_CORE
    y = N_YLO * y_hi + y_lo
    way = 1 - 2 * core
    odd, pair = x % 2, x // 2

    def device(dz, dx, dy):
        x_to, y_to, z_to = (x + dx + N_X) % N_X, (y + dy + N_Y) % N_Y, (z + dz + N_Z) % N_Z
        return (y_to % N_YLO) * N_Z + z_to, (x_to * N_YHI + y_to // N_YLO) * N_CORE + core

    def to(k):
        return device(*(way * d for d in OFFSETS[k]))

    def back(k):
        return device(*(-way * d for d in OFFSETS[k]))

    def slab_of(k):
        dz, dx, dy = (way * d for d in OFFSETS[k])
        return ((y + dy + N_Y) % N_YLO) * N_Z + (z + dz + N_Z + FAR * ((x + dx + N_X) % 2)) % N_Z

    def y_peer(d):
        return device(0, 0, N_YLO * d)

    x_peer = device(0, 2, 0)
    sibling = (slab, group + way)
    near, across, beyond = device(0, 1 - 2 * odd, 0), device(FAR, 1 - 2 * odd, 0), device(FAR, 0, 0)

    def choose(a, b):
        return tuple(odd * v + (1 - odd) * u for u, v in zip(a, b))

    def copy(src, dst, send, recv, device):
        return pltpu.make_async_remote_copy(
            src_ref=src, dst_ref=dst, send_sem=send, recv_sem=recv, device_id=device, device_id_type=MESH
        )

    loads = [
        pltpu.make_async_copy(a, b, s_in.at[i])
        for i, (a, b) in enumerate(((own_hbm, own), (ids_hbm, ids), (ctf_hbm, ctf), (refs_hbm, refs), (img_hbm, img)))
    ]
    for c in loads:
        c.start()

    barrier = pltpu.get_barrier_semaphore()
    partners = [back(k) for k in range(1, n)]
    partners += [y_peer(d) for d in range(1, N_YHI)] + [x_peer, sibling, near, across]
    for p in partners:
        pl.semaphore_signal(barrier, inc=1, device_id=p, device_id_type=MESH)

    @pl.when(odd == 1)
    def _():
        pl.semaphore_signal(barrier, inc=1, device_id=beyond, device_id_type=MESH)

    for c in loads[:3]:
        c.wait()

    target = iota((n, rows), 0)
    wanted = jnp.zeros((n, rows), jnp.int32)
    for k in range(n):
        wanted = jnp.where(target == k, slab_of(k), wanted)
    hot = (wanted == own[...]).astype(F32)
    hot_b = hot.astype(BF16)
    before = (iota((rows, rows), 0) < iota((rows, rows), 1)).astype(F32).astype(BF16)
    rank = jnp.sum(hot * nn(hot_b, before), axis=0, keepdims=True)
    line_k = jnp.sum(hot * target.astype(F32), axis=0, keepdims=True)
    slot = (line_k * cap + rank).astype(jnp.int32)
    tag_row = (ids[...] + 1).astype(F32)
    rank_hot = (iota((128, rows), 0) == rank.astype(jnp.int32)).astype(F32).astype(BF16)
    tag_slots = nt((hot * tag_row).astype(BF16), rank_hot)
    for k in range(n):
        send_tags[k] = jnp.broadcast_to(tag_slots[k : k + 1, :], (8, 128))

    pl.semaphore_wait(barrier, len(partners) + odd)
    loads[3].wait()

    slot_ref = ref_all.at[core, pair, y_hi, odd]
    ag = copy(refs, slot_ref, s_ag.at[0], r_ag.at[odd], choose(across, near))
    ag.start()
    ag_2 = copy(refs, slot_ref, s_ag.at[1], r_ag.at[1], beyond)

    @pl.when(odd == 1)
    def _():
        ag_2.start()

    @pl.when(odd == 0)
    def _():
        ref_all[core, pair, y_hi, 0] = refs[...]

    pick = (iota((groups, rows), 0) == ids[...]).astype(F32).astype(BF16)
    ctf_hi, ctf_mid, ctf_lo = three(ctf[...])
    ctf_rows = tn(pick, ctf_hi) + tn(pick, ctf_mid) + tn(pick, ctf_lo)
    loads[4].wait()
    weighted[:, :half] = (img[:, :half].astype(F32) * ctf_rows).astype(BF16)
    weighted[:, half:] = (img[:, half:].astype(F32) * ctf_rows).astype(BF16)

    @pl.when(odd == 1)
    def _():
        copy(refs, ref_all.at[core, pair, y_hi, 0], s_ag.at[0], r_ag.at[0], across).wait_recv()
        ag_2.wait_send()

    copy(refs, ref_all.at[core, pair, y_hi, 1], s_ag.at[0], r_ag.at[1], across).wait_recv()
    mine = ref_all.at[core, pair, y_hi]
    ag_y = [copy(mine, mine, s_agy.at[d - 1], r_agy.at[d - 1], y_peer(d)) for d in range(1, N_YHI)]
    for c in ag_y:
        c.start()
    sends = []
    for b in reversed(range(batches)):
        place = (iota((span, rows), 0) + b * span == slot).astype(F32).astype(BF16)
        packed = nn(place, weighted[...]).astype(BF16)
        for j in reversed(range(PER_BATCH)):
            k = b * PER_BATCH + j
            part = packed[j * cap : (j + 1) * cap]
            if k == 0:
                lines[0] = part
                tags[0] = send_tags[0]
                continue
            send_lines[k] = part
            line_copy = copy(send_lines.at[k], lines.at[k], s_line.at[k], r_line.at[k], to(k))
            tag_copy = copy(send_tags.at[k], tags.at[k], s_tag.at[k], r_tag.at[k], to(k))
            tag_copy.start()
            line_copy.start()
            sends += [tag_copy, line_copy]

    k_loc = N_CORE * N_X * N_YHI * per
    ctf_sq = ctf[...] * ctf[...]
    ctf_sq4 = jnp.concatenate([ctf_sq] * (128 // groups), axis=0).astype(BF16)
    p_rows = k_loc // 4

    def set_quad(c, p):
        reference = ref_all[c, p].reshape(p_rows, width)
        re, im = reference[:, :half].astype(F32), reference[:, half:].astype(F32)
        power = (re * re + im * im).astype(BF16)
        hi, mid, lo = three(-0.5 * nt(power, ctf_sq4))
        lane = iota((p_rows, 128), 1)
        parts = jnp.where(lane < 2 * groups, mid.astype(F32), jnp.where(lane < 3 * groups, lo.astype(F32), 0.0))
        quad[c, p] = jnp.where(lane < groups, hi.astype(F32), parts).astype(BF16)

    for c in ag_y:
        c.wait_recv()
    mine, theirs = ref_all.at[core, pair], ref_all.at[core, 1 - pair]
    ag_x = [copy(mine, mine, s_agx, r_agx, x_peer)]
    ag_x[0].start()
    ag_c = [copy(p, p, s_agc.at[i], r_agc.at[i], sibling) for i, p in enumerate((mine, theirs))]
    ag_c[0].start()
    set_quad(core, pair)
    ag_c[0].wait_recv()
    set_quad(1 - core, pair)
    ag_x[0].wait_recv()
    ag_c[1].start()
    set_quad(core, 1 - pair)
    ag_c[1].wait_recv()
    set_quad(1 - core, 1 - pair)
    sends += [ag] + ag_y + ag_x + ag_c

    scale = width**-0.5
    spread = (iota((128, span), 0) == iota((128, span), 1) % cap).astype(F32).astype(BF16)
    mine_8 = (iota((PER_BATCH * 8, span), 0) == 8 * (iota((PER_BATCH * 8, span), 1) // cap)).astype(F32)
    tag_of = (iota((128, span), 0) % groups + 1).astype(F32)
    ev_sends = []
    for b in range(batches):
        for j in range(PER_BATCH):
            k = b * PER_BATCH + j
            if k:
                copy(send_tags.at[k], tags.at[k], s_tag.at[k], r_tag.at[k], to(k)).wait_recv()
                copy(send_lines.at[k], lines.at[k], s_line.at[k], r_line.at[k], to(k)).wait_recv()
        here = slice(b * span, (b + 1) * span)
        batch = lines[b * PER_BATCH : (b + 1) * PER_BATCH].reshape(span, width)
        tag8 = tags[b * PER_BATCH : (b + 1) * PER_BATCH].reshape(PER_BATCH * 8, 128).astype(BF16)
        tag = jnp.sum(nn(tag8, spread) * mine_8, axis=0, keepdims=True)
        pick = (tag_of == tag).astype(F32).astype(BF16)
        chosen[:, here] = pick
        score = nt(ref_all[...].reshape(k_loc, width), batch) + nn(quad[...].reshape(k_loc, 128), pick)
        score *= scale
        top = jnp.max(score, axis=0, keepdims=True)
        e = jnp.exp(score - top)
        total = jnp.sum(e, axis=0, keepdims=True)
        resp[:, here] = (e * (1.0 / total)).astype(BF16)
        send_ev[b] = jnp.broadcast_to(top + jnp.log(total), (8, span))
        for j in range(PER_BATCH):
            k = b * PER_BATCH + j
            if k:
                ev_copy = copy(send_ev.at[b], ev.at[k], s_ev.at[k], r_ev.at[k], back(k))
                ev_copy.start()
                ev_sends.append(ev_copy)
            else:
                ev[0] = send_ev[0]

    h_rows = k_loc // N_CORE
    x_rows = h_rows // 2
    own_lanes = iota((h_rows, 128), 1) // groups == (iota((h_rows, 128), 0) // 8) % (2 * per // 8)

    def sum_half(c):
        r = resp[pl.ds(pl.multiple_of(c * h_rows, h_rows), h_rows), :]
        acc[c] = nn(r, lines[...].reshape(n * cap, width))
        count = jnp.where(own_lanes, nt(r, chosen[...]), 0.0)
        return jnp.sum(count.reshape(2, N_YHI, 2 * per // 8, 8, 128), axis=2)

    rcore_out[...] = sum_half(1 - core)
    core_sends = [copy(rcore_out, rcore_in, s_rcc, r_rcc, sibling)]
    for i, xp in enumerate((1 - pair, pair)):
        at = pl.ds(pl.multiple_of(xp * x_rows, x_rows), x_rows)
        core_sends.append(copy(acc.at[1 - core, at], core_in.at[at], s_rsc.at[i], r_rsc.at[i], sibling))
    for c in core_sends:
        c.start()
    racc[...] = sum_half(core)

    core_sends[0].wait_recv()
    rx_out[...] = racc[...] + rcore_in[...]
    x_sends = []
    for i, xp in enumerate((1 - pair, pair)):
        at = pl.ds(pl.multiple_of(xp * x_rows, x_rows), x_rows)
        core_sends[1 + i].wait_recv()
        both = acc[core, at] + core_in[at]
        if i:
            own_rows[...] = both
            continue
        x_out[...] = both.astype(BF16)
        xc = copy(x_out, x_in, s_rsx, r_rsx, x_peer)
        rc = copy(rx_out.at[xp], rx_in, s_rcx, r_rcx, x_peer)
        rc.start()
        xc.start()
        x_sends += [rc, xc]
    for c in x_sends:
        c.wait_recv()
    own_cnt = rx_out[pair] + rx_in[...]

    ry_out[...] = own_cnt
    y_sends = []
    for d in (2, 1, 3):
        at = pl.ds(pl.multiple_of(((y_hi + d) % N_YHI) * 2 * per, 2 * per), 2 * per)
        y_out[d - 1] = (own_rows[at] + x_in[at].astype(F32)).astype(BF16)
        yc = copy(y_out.at[d - 1], y_in.at[d - 1], s_rsy.at[d - 1], r_rsy.at[d - 1], y_peer(d))
        rc = copy(ry_out.at[(y_hi + d) % N_YHI], ry_in.at[d - 1], s_rcy.at[d - 1], r_rcy.at[d - 1], y_peer(d))
        rc.start()
        yc.start()
        y_sends += [rc, yc]

    for c in ev_sends:
        c.wait_recv()
    at_lane = line_k - PER_BATCH * jnp.floor(line_k * (1.0 / PER_BATCH))
    lane_hot = (iota((span, rows), 0) == (at_lane * cap + rank).astype(jnp.int32)).astype(F32).astype(BF16)
    e_hi, e_mid, e_lo = three(ev[:, 0, :])
    by_target = nn(e_hi, lane_hot) + nn(e_mid, lane_hot) + nn(e_lo, lane_hot)
    line_ev[...] = jnp.sum(hot * by_target, axis=0, keepdims=True)

    at = pl.ds(pl.multiple_of(y_hi * 2 * per, 2 * per), 2 * per)
    part = own_rows[at] + x_in[at].astype(F32)
    for c in y_sends:
        c.wait_recv()
    count = ry_out[y_hi]
    for d in range(1, N_YHI):
        part += y_in[d - 1].astype(F32)
        count += ry_in[d - 1]
    fin_out[...] = part.reshape(2, per, width).astype(BF16)
    rfin_out[...] = count

    def fins(src, dst, i, dev):
        return (
            copy(rfin_out, rfin_in.at[dst], s_rfin.at[i], r_rfin.at[dst], dev),
            copy(fin_out.at[src], fin_in.at[dst], s_fin.at[i], r_fin.at[dst], dev),
        )

    fin = fins(1 - odd, odd, 0, choose(near, across))
    fin_2 = fins(1, 1, 1, beyond)
    for c in fin:
        c.start()

    @pl.when(odd == 1)
    def _():
        for c in fin_2:
            c.start()
        for c in fins(0, 0, 0, near):
            c.wait_recv()

    @pl.when(odd == 0)
    def _():
        fin_in[0] = fin_out[0]
        rfin_in[0] = rfin_out[...]

    for c in fins(0, 1, 0, near):
        c.wait_recv()
    final = fin_in[0].astype(F32) + fin_in[1].astype(F32)
    tile = rfin_in[0] + rfin_in[1]
    cnt = jnp.concatenate([tile] * (per // 8), axis=0)
    cnt = jnp.where(iota((per, 128), 1) // groups == iota((per, 128), 0) // 8 + odd * (per // 8), cnt, 0.0)
    c_hi, c_mid, c_lo = three(cnt)
    den = nn(c_hi, ctf_sq4) + nn(c_mid, ctf_sq4) + nn(c_lo, ctf_sq4) + 1.0
    out[:, :half] = final[:, :half] / den
    out[:, half:] = final[:, half:] / den

    @pl.when(odd == 1)
    def _():
        for c in fin_2:
            c.wait_send()

    for c in sends + ev_sends + core_sends + x_sends + y_sends + list(fin):
        c.wait_send()


def on_device(images, references, ctf_table, ctf_ids, owners):
    rows, width = images.shape
    per = references.shape[0]
    n = len(OFFSETS)
    cap = 3 * rows // n
    h_rows = N_X * N_YHI * per
    x_rows = h_rows // 2
    dma = pltpu.SemaphoreType.DMA
    vm = pltpu.VMEM
    scratch = [
        vm((rows, width), BF16), vm((per, width), BF16), vm(ctf_table.shape, F32),
        vm((1, rows), jnp.int32), vm((1, rows), jnp.int32),
        vm((rows, width), BF16), vm((n, cap, width), BF16), vm((n, cap, width), BF16),
        vm((n, 8, 128), F32), vm((n, 8, 128), F32),
        vm((n // PER_BATCH, 8, PER_BATCH * cap), F32), vm((n, 8, PER_BATCH * cap), F32),
        vm((N_CORE, 2, N_YHI, 2, per, width), BF16), vm((N_CORE * h_rows, n * cap), BF16), vm((128, n * cap), BF16),
        vm((N_CORE, 2, x_rows, 128), BF16), vm((N_CORE, h_rows, width), F32), vm((2, N_YHI, 8, 128), F32),
        vm((h_rows, width), F32), vm((2, N_YHI, 8, 128), F32), vm((2, N_YHI, 8, 128), F32),
        vm((x_rows, width), BF16), vm((x_rows, width), BF16), vm((2, N_YHI, 8, 128), F32), vm((N_YHI, 8, 128), F32),
        vm((x_rows, width), F32),
        vm((N_YHI - 1, 2 * per, width), BF16), vm((N_YHI - 1, 2 * per, width), BF16),
        vm((N_YHI, 8, 128), F32), vm((N_YHI - 1, 8, 128), F32),
        vm((2, per, width), BF16), vm((2, per, width), BF16), vm((8, 128), F32), vm((2, 8, 128), F32),
        dma((5,)),
        *[dma((n,))] * 6,
        *[dma((2,))] * 2, *[dma((N_YHI - 1,))] * 2, *[dma] * 2, *[dma((2,))] * 2,
        *[dma((2,))] * 2, *[dma] * 6, *[dma((N_YHI - 1,))] * 4,
        *[dma((2,))] * 4,
    ]
    new, ev = pl.pallas_call(
        kernel,
        out_shape=(jax.ShapeDtypeStruct((per, width), F32), jax.ShapeDtypeStruct((1, rows), F32)),
        in_specs=[pl.BlockSpec(memory_space=pltpu.HBM)] * 5,
        out_specs=[pl.BlockSpec(memory_space=pltpu.VMEM)] * 2,
        scratch_shapes=scratch,
        compiler_params=pltpu.CompilerParams(
            collective_id=0, has_side_effects=True, vmem_limit_bytes=48 * 2**20
        ),
    )(images, references, ctf_table, ctf_ids.reshape(1, rows), owners.reshape(1, rows))
    return new, ev.reshape(rows)


def solution(mesh):
    both = P(("slab", "group"))
    rows = P(("slab", "group"), None)
    return jax.shard_map(
        on_device, mesh=mesh, in_specs=(rows, rows, P(), both, both), out_specs=(rows, both), check_vma=False
    )
```

time: 75 us -> 67.4 us (0.90)
  the two profiles are of different devices: /device:TPU:2 before, /device:TPU:64 now
where the time goes in v3:
time: 67.4 us; the launch traced here: 67.1 us
  Pallas kernels  62 us (92%)
  local copies, waits for them, and re-layouts  4.39 us (7%)
    pallas_call x1, Pallas kernels, on_device(): pl.pallas_call(kernel, out_shape=(jax.ShapeDtypeStruct((per, width), F32)...  62 us
    unnamed x12, local copies, waits for them, and re-layouts  4.39 us

profile of v3, /device:TPU:64, one launch (start us, length us, event | category | flops | bytes accessed | tf_op | source)
XLA Modules:
  0.0 67.1 jit_solution(10482316737735540618)
XLA Ops:
  0.6 0.0 copy-start.4
  0.6 0.0 copy-start.3
  0.7 0.7 copy-done.4
  1.3 0.0 copy-done.3
  1.3 0.0 copy-start
  1.3 1.0 %copy-done = bf16[256,768]{1,0:T(8,128)(2,1)S(1)} copy-done((bf16[256,768]{1,0:T(8,128)(2,1)S(1)}, bf16[256,768]{1,0:T(8,128)(2,1)}, u32[]{:S(2)}) %copy-start) | copy-done | bytes 393240
  2.3 0.0 copy-start.1
  2.3 0.8 %copy-done.1 = f32[32,384]{1,0:T(8,128)S(1)} copy-done((f32[32,384]{1,0:T(8,128)S(1)}, f32[32,384]{1,0:T(8,128)}, u32[]{:S(2)}) %copy-start.1) | copy-done | bytes 49176
  3.1 0.0 copy-start.2
  3.1 0.7 %copy-done.2 = bf16[16,768]{1,0:T(8,128)(2,1)S(1)} copy-done((bf16[16,768]{1,0:T(8,128)(2,1)S(1)}, bf16[16,768]{1,0:T(8,128)(2,1)}, u32[]{:S(2)}) %copy-start.2) | copy-done | bytes 24600
  3.9 62.0 %shard_map.68 = (f32[16,768]{1,0:T(8,128)S(1)}, f32[1,256]{1,0:T(1,128)S(1)}) custom-call(bf16[256,768]{1,0:T(8,128)(2,1)S(1)} %copy-done, bf16[16,768]{1,0:T(8,128)(2,1)S(1)} %copy-done.2, f32[32,384]{1,0:T(8,128)S(1)} %copy-done.1, s32[1,256]{1,0:T(1,128)S(1)} %bitcast.3, s32[1,256]{1,0:T(1,128)S(1)} %bitcast.4), custom_call_target="tpu_custom_call" | custom-call | tf_op jit(solution)/shard_map/pallas_call | solution.py:392
  65.9 0.6 copy.9
  66.5 0.6 copy.10
Async XLA Ops:
  0.6 0.7 %copy-start.4 = (s32[256]{0:T(256)S(1)}, s32[256]{0:T(256)}, u32[]{:S(2)}) copy-start(s32[256]{0:T(256)} %param.9) | copy-start | bytes 3076
  0.6 0.7 %copy-start.3 = (s32[256]{0:T(256)S(1)}, s32[256]{0:T(256)}, u32[]{:S(2)}) copy-start(s32[256]{0:T(256)} %param.8) | copy-start | bytes 3076
  1.3 1.0 %copy-start = (bf16[256,768]{1,0:T(8,128)(2,1)S(1)}, bf16[256,768]{1,0:T(8,128)(2,1)}, u32[]{:S(2)}) copy-start(bf16[256,768]{1,0:T(8,128)(2,1)} %img_hbm.1) | copy-start | bytes 1179652
  2.3 0.8 %copy-start.1 = (f32[32,384]{1,0:T(8,128)S(1)}, f32[32,384]{1,0:T(8,128)}, u32[]{:S(2)}) copy-start(f32[32,384]{1,0:T(8,128)} %ctf_hbm.1) | copy-start | bytes 147460
  3.1 0.7 %copy-start.2 = (bf16[16,768]{1,0:T(8,128)(2,1)S(1)}, bf16[16,768]{1,0:T(8,128)(2,1)}, u32[]{:S(2)}) copy-start(bf16[16,768]{1,0:T(8,128)(2,1)} %refs_hbm.1) | copy-start | bytes 73732

commit v4 on v3

--- a/solution.py
+++ b/solution.py
@@ -166,6 +166,10 @@
     ag_y = [copy(mine, mine, s_agy.at[d - 1], r_agy.at[d - 1], y_peer(d)) for d in range(1, N_YHI)]
     for c in ag_y:
         c.start()
+    blocks = [ref_all.at[core, pair, (y_hi + N_YHI - d) % N_YHI] for d in range(N_YHI)]
+    ag_x = [copy(p, p, s_agx.at[d], r_agx.at[d], x_peer) for d, p in enumerate(blocks)]
+    ag_x[0].start()
+
     sends = []
     for b in reversed(range(batches)):
         place = (iota((span, rows), 0) + b * span == slot).astype(F32).astype(BF16)
@@ -198,17 +202,17 @@
         parts = jnp.where(lane < 2 * groups, mid.astype(F32), jnp.where(lane < 3 * groups, lo.astype(F32), 0.0))
         quad[c, p] = jnp.where(lane < groups, hi.astype(F32), parts).astype(BF16)
 
-    for c in ag_y:
-        c.wait_recv()
+    for d in (1, 3, 2):
+        ag_y[d - 1].wait_recv()
+        ag_x[d].start()
     mine, theirs = ref_all.at[core, pair], ref_all.at[core, 1 - pair]
-    ag_x = [copy(mine, mine, s_agx, r_agx, x_peer)]
-    ag_x[0].start()
     ag_c = [copy(p, p, s_agc.at[i], r_agc.at[i], sibling) for i, p in enumerate((mine, theirs))]
     ag_c[0].start()
     set_quad(core, pair)
     ag_c[0].wait_recv()
     set_quad(1 - core, pair)
-    ag_x[0].wait_recv()
+    for c in ag_x:
+        c.wait_recv()
     ag_c[1].start()
     set_quad(core, 1 - pair)
     ag_c[1].wait_recv()
@@ -238,7 +242,7 @@
         e = jnp.exp(score - top)
         total = jnp.sum(e, axis=0, keepdims=True)
         resp[:, here] = (e * (1.0 / total)).astype(BF16)
-        send_ev[b] = jnp.broadcast_to(top + jnp.log(total), (8, span))
+        send_ev[b] = top + jnp.log(total)
         for j in range(PER_BATCH):
             k = b * PER_BATCH + j
             if k:
@@ -269,34 +273,40 @@
 
     core_sends[0].wait_recv()
     rx_out[...] = racc[...] + rcore_in[...]
+    rc = copy(rx_out.at[1 - pair], rx_in, s_rcx, r_rcx, x_peer)
+    rc.start()
     x_sends = []
-    for i, xp in enumerate((1 - pair, pair)):
-        at = pl.ds(pl.multiple_of(xp * x_rows, x_rows), x_rows)
-        core_sends[1 + i].wait_recv()
-        both = acc[core, at] + core_in[at]
-        if i:
-            own_rows[...] = both
-            continue
-        x_out[...] = both.astype(BF16)
-        xc = copy(x_out, x_in, s_rsx, r_rsx, x_peer)
-        rc = copy(rx_out.at[xp], rx_in, s_rcx, r_rcx, x_peer)
-        rc.start()
-        xc.start()
-        x_sends += [rc, xc]
-    for c in x_sends:
-        c.wait_recv()
+    turns = (2, 1, 3, 0)
+    core_sends[1].wait_recv()
+
+    def rows_of(d, first=0):
+        at = first + ((y_hi + d) % N_YHI) * 2 * per
+        return pl.ds(pl.multiple_of(at, 2 * per), 2 * per)
+
+    for i, d in enumerate(turns):
+        at, far_at = rows_of(d), rows_of(d, (1 - pair) * x_rows)
+        x_out[at] = (acc[core, far_at] + core_in[far_at]).astype(BF16)
+        x_sends.append(copy(x_out.at[at], x_in.at[at], s_rsx.at[i], r_rsx.at[i], x_peer))
+        x_sends[-1].start()
+    core_sends[2].wait_recv()
+    near_at = pl.ds(pl.multiple_of(pair * x_rows, x_rows), x_rows)
+    own_rows[...] = acc[core, near_at] + core_in[near_at]
+
+    rc.wait_recv()
     own_cnt = rx_out[pair] + rx_in[...]
-
     ry_out[...] = own_cnt
     y_sends = []
-    for d in (2, 1, 3):
-        at = pl.ds(pl.multiple_of(((y_hi + d) % N_YHI) * 2 * per, 2 * per), 2 * per)
+    for i, d in enumerate(turns[:-1]):
+        x_sends[i].wait_recv()
+        at = rows_of(d)
         y_out[d - 1] = (own_rows[at] + x_in[at].astype(F32)).astype(BF16)
         yc = copy(y_out.at[d - 1], y_in.at[d - 1], s_rsy.at[d - 1], r_rsy.at[d - 1], y_peer(d))
-        rc = copy(ry_out.at[(y_hi + d) % N_YHI], ry_in.at[d - 1], s_rcy.at[d - 1], r_rcy.at[d - 1], y_peer(d))
-        rc.start()
+        rcy = copy(ry_out.at[(y_hi + d) % N_YHI], ry_in.at[d - 1], s_rcy.at[d - 1], r_rcy.at[d - 1], y_peer(d))
+        rcy.start()
         yc.start()
-        y_sends += [rc, yc]
+        y_sends += [rcy, yc]
+    x_sends[-1].wait_recv()
+    x_sends.append(rc)
 
     for c in ev_sends:
         c.wait_recv()
@@ -306,7 +316,7 @@
     by_target = nn(e_hi, lane_hot) + nn(e_mid, lane_hot) + nn(e_lo, lane_hot)
     line_ev[...] = jnp.sum(hot * by_target, axis=0, keepdims=True)
 
-    at = pl.ds(pl.multiple_of(y_hi * 2 * per, 2 * per), 2 * per)
+    at = rows_of(0)
     part = own_rows[at] + x_in[at].astype(F32)
     for c in y_sends:
         c.wait_recv()
@@ -374,7 +384,7 @@
         vm((1, rows), jnp.int32), vm((1, rows), jnp.int32),
         vm((rows, width), BF16), vm((n, cap, width), BF16), vm((n, cap, width), BF16),
         vm((n, 8, 128), F32), vm((n, 8, 128), F32),
-        vm((n // PER_BATCH, 8, PER_BATCH * cap), F32), vm((n, 8, PER_BATCH * cap), F32),
+        vm((n // PER_BATCH, 1, PER_BATCH * cap), F32), vm((n, 1, PER_BATCH * cap), F32),
         vm((N_CORE, 2, N_YHI, 2, per, width), BF16), vm((N_CORE * h_rows, n * cap), BF16), vm((128, n * cap), BF16),
         vm((N_CORE, 2, x_rows, 128), BF16), vm((N_CORE, h_rows, width), F32), vm((2, N_YHI, 8, 128), F32),
         vm((h_rows, width), F32), vm((2, N_YHI, 8, 128), F32), vm((2, N_YHI, 8, 128), F32),
@@ -385,8 +395,8 @@
         vm((2, per, width), BF16), vm((2, per, width), BF16), vm((8, 128), F32), vm((2, 8, 128), F32),
         dma((5,)),
         *[dma((n,))] * 6,
-        *[dma((2,))] * 2, *[dma((N_YHI - 1,))] * 2, *[dma] * 2, *[dma((2,))] * 2,
-        *[dma((2,))] * 2, *[dma] * 6, *[dma((N_YHI - 1,))] * 4,
+        *[dma((2,))] * 2, *[dma((N_YHI - 1,))] * 2, *[dma((N_YHI,))] * 2, *[dma((2,))] * 2,
+        *[dma((2,))] * 2, *[dma] * 2, *[dma((N_YHI,))] * 2, *[dma] * 2, *[dma((N_YHI - 1,))] * 4,
         *[dma((2,))] * 4,
     ]
     new, ev = pl.pallas_call(
@@ -396,7 +406,7 @@
         out_specs=[pl.BlockSpec(memory_space=pltpu.VMEM)] * 2,
         scratch_shapes=scratch,
         compiler_params=pltpu.CompilerParams(
-            collective_id=0, has_side_effects=True, vmem_limit_bytes=48 * 2**20
+            collective_id=0, has_side_effects=True, vmem_limit_bytes=62 * 2**20
         ),
     )(images, references, ctf_table, ctf_ids.reshape(1, rows), owners.reshape(1, rows))
     return new, ev.reshape(rows)

time: 67.4 us -> 62 us (0.920)
  the two profiles are of different devices: /device:TPU:64 before, /device:TPU:1 now
where the time goes in v4:
time: 62 us; the launch traced here: 61.5 us
  Pallas kernels  58.9 us (95%)
  local copies, waits for them, and re-layouts  1.99 us (3%)
  between operations  0.65 us (1%)
    pallas_call x1, Pallas kernels, on_device(): pl.pallas_call(kernel, out_shape=(jax.ShapeDtypeStruct((per, width), F32)...  58.9 us
    unnamed x4, local copies, waits for them, and re-layouts  1.99 us

profile of v4, /device:TPU:1, one launch (start us, length us, event | category | flops | bytes accessed | tf_op | source)
XLA Modules:
  0.0 61.5 jit_solution(8187320004114314913)
XLA Ops:
  0.6 58.9 %shard_map.68 = (f32[16,768]{1,0:T(8,128)}, f32[1,256]{1,0:T(1,128)}) custom-call(bf16[256,768]{1,0:T(8,128)(2,1)} %img_hbm.1, bf16[16,768]{1,0:T(8,128)(2,1)} %refs_hbm.1, f32[32,384]{1,0:T(8,128)} %ctf_hbm.1, s32[1,256]{1,0:T(1,128)} %bitcast.3, s32[1,256]{1,0:T(1,128)} %bitcast.4), custom_call_target="tpu_custom_call" | custom-call | tf_op jit(solution)/shard_map/pallas_call | solution.py:402
  59.5 0.0 copy-start
  59.5 1.4 %copy.9 = f32[16,768]{1,0:T(8,128)} copy(f32[16,768]{1,0:T(8,128)} %get-tuple-element.8) | data formatting | bytes 98304
  60.9 0.0 copy-done
  60.9 0.6 copy.10
Async XLA Ops:
  59.5 1.4 %copy-start = (f32[1,256]{1,0:T(1,128)S(1)}, f32[1,256]{1,0:T(1,128)}, u32[]{:S(2)}) copy-start(f32[1,256]{1,0:T(1,128)} %get-tuple-element.5) | copy-start | bytes 3076

commit v5 on v4

--- a/solution.py
+++ b/solution.py
@@ -133,28 +133,49 @@
     for k in range(n):
         send_tags[k] = jnp.broadcast_to(tag_slots[k : k + 1, :], (8, 128))
 
-    pl.semaphore_wait(barrier, len(partners) + odd)
-    loads[3].wait()
-
-    slot_ref = ref_all.at[core, pair, y_hi, odd]
-    ag = copy(refs, slot_ref, s_ag.at[0], r_ag.at[odd], choose(across, near))
-    ag.start()
-    ag_2 = copy(refs, slot_ref, s_ag.at[1], r_ag.at[1], beyond)
-
-    @pl.when(odd == 1)
-    def _():
-        ag_2.start()
-
-    @pl.when(odd == 0)
-    def _():
-        ref_all[core, pair, y_hi, 0] = refs[...]
-
     pick = (iota((groups, rows), 0) == ids[...]).astype(F32).astype(BF16)
     ctf_hi, ctf_mid, ctf_lo = three(ctf[...])
     ctf_rows = tn(pick, ctf_hi) + tn(pick, ctf_mid) + tn(pick, ctf_lo)
     loads[4].wait()
     weighted[:, :half] = (img[:, :half].astype(F32) * ctf_rows).astype(BF16)
     weighted[:, half:] = (img[:, half:].astype(F32) * ctf_rows).astype(BF16)
+
+    for b in range(batches):
+        place = (iota((span, rows), 0) + b * span == slot).astype(F32).astype(BF16)
+        send_lines[b * PER_BATCH : (b + 1) * PER_BATCH] = (
+            nn(place, weighted[...]).astype(BF16).reshape(PER_BATCH, cap, width)
+        )
+    lines[0] = send_lines[0]
+    tags[0] = send_tags[0]
+
+    pl.semaphore_wait(barrier, len(partners) + odd)
+    loads[3].wait()
+
+    slot_ref = ref_all.at[core, pair, y_hi, odd]
+    ag = copy(refs, slot_ref, s_ag.at[0], r_ag.at[odd], choose(across, near))
+    ag.start()
+    ag_2 = copy(refs, slot_ref, s_ag.at[1], r_ag.at[1], beyond)
+
+    @pl.when(odd == 1)
+    def _():
+        ag_2.start()
+
+    @pl.when(odd == 0)
+    def _():
+        ref_all[core, pair, y_hi, 0] = refs[...]
+
+    sends = []
+
+    def send_slots(k):
+        line_copy = copy(send_lines.at[k], lines.at[k], s_line.at[k], r_line.at[k], to(k))
+        tag_copy = copy(send_tags.at[k], tags.at[k], s_tag.at[k], r_tag.at[k], to(k))
+        tag_copy.start()
+        line_copy.start()
+        return [tag_copy, line_copy]
+
+    for k in reversed(range(1, n)):
+        if OFFSETS[k][2] == 0:
+            sends += send_slots(k)
 
     @pl.when(odd == 1)
     def _():
@@ -170,23 +191,9 @@
     ag_x = [copy(p, p, s_agx.at[d], r_agx.at[d], x_peer) for d, p in enumerate(blocks)]
     ag_x[0].start()
 
-    sends = []
-    for b in reversed(range(batches)):
-        place = (iota((span, rows), 0) + b * span == slot).astype(F32).astype(BF16)
-        packed = nn(place, weighted[...]).astype(BF16)
-        for j in reversed(range(PER_BATCH)):
-            k = b * PER_BATCH + j
-            part = packed[j * cap : (j + 1) * cap]
-            if k == 0:
-                lines[0] = part
-                tags[0] = send_tags[0]
-                continue
-            send_lines[k] = part
-            line_copy = copy(send_lines.at[k], lines.at[k], s_line.at[k], r_line.at[k], to(k))
-            tag_copy = copy(send_tags.at[k], tags.at[k], s_tag.at[k], r_tag.at[k], to(k))
-            tag_copy.start()
-            line_copy.start()
-            sends += [tag_copy, line_copy]
+    for k in reversed(range(1, n)):
+        if OFFSETS[k][2]:
+            sends += send_slots(k)
 
     k_loc = N_CORE * N_X * N_YHI * per
     ctf_sq = ctf[...] * ctf[...]

time: 62 us -> 60.9 us (0.982)
  the two profiles are of different devices: /device:TPU:1 before, /device:TPU:8 now
where the time goes in v5:
time: 60.9 us; the launch traced here: 60.7 us
  Pallas kernels  58 us (95%)
  local copies, waits for them, and re-layouts  1.99 us (3%)
  between operations  0.65 us (1%)
    pallas_call x1, Pallas kernels, on_device(): pl.pallas_call(kernel, out_shape=(jax.ShapeDtypeStruct((per, width), F32)...  58 us
    unnamed x4, local copies, waits for them, and re-layouts  1.99 us

profile of v5, /device:TPU:8, one launch (start us, length us, event | category | flops | bytes accessed | tf_op | source)
XLA Modules:
  0.0 60.7 jit_solution(12336255800098589923)
XLA Ops:
  0.6 58.0 %shard_map.68 = (f32[16,768]{1,0:T(8,128)}, f32[1,256]{1,0:T(1,128)}) custom-call(bf16[256,768]{1,0:T(8,128)(2,1)} %img_hbm.1, bf16[16,768]{1,0:T(8,128)(2,1)} %refs_hbm.1, f32[32,384]{1,0:T(8,128)} %ctf_hbm.1, s32[1,256]{1,0:T(1,128)} %bitcast.3, s32[1,256]{1,0:T(1,128)} %bitcast.4), custom_call_target="tpu_custom_call" | custom-call | tf_op jit(solution)/shard_map/pallas_call | solution.py:409
  58.7 0.0 copy-start
  58.7 1.4 %copy.9 = f32[16,768]{1,0:T(8,128)} copy(f32[16,768]{1,0:T(8,128)} %get-tuple-element.8) | data formatting | bytes 98304
  60.1 0.0 copy-done
  60.1 0.6 copy.10
Async XLA Ops:
  58.7 1.4 %copy-start = (f32[1,256]{1,0:T(1,128)S(1)}, f32[1,256]{1,0:T(1,128)}, u32[]{:S(2)}) copy-start(f32[1,256]{1,0:T(1,128)} %get-tuple-element.5) | copy-start | bytes 3076

commit v6 on v5

--- a/solution.py
+++ b/solution.py
@@ -47,6 +47,7 @@
     ref_all, resp, chosen, quad, acc, racc,
     core_in, rcore_out, rcore_in, x_out, x_in, rx_out, rx_in, own_rows, y_out, y_in, ry_out, ry_in,
     fin_out, fin_in, rfin_out, rfin_in,
+    ctf_sq4, spread, owner_row, tag_of, own_lanes, lane_hot, hot_lines,
     s_in,
     s_line, r_line, s_tag, r_tag, s_ev, r_ev,
     s_ag, r_ag, s_agy, r_agy, s_agx, r_agx, s_agc, r_agc,
@@ -62,32 +63,58 @@
     batches = n // PER_BATCH
     span = PER_BATCH * cap
     slab, group = lax.axis_index("slab"), lax.axis_index("group")
-    y_lo, z = slab // N_Z, slab % N_Z
-    x, y_hi, core = group // (N_YHI * N_CORE), (group // N_CORE) % N_YHI, group % N_CORE
+    y_lo, z = lax.div(slab, N_Z), lax.rem(slab, N_Z)
+    x, core = lax.div(group, N_YHI * N_CORE), lax.rem(group, N_CORE)
+    y_hi = lax.rem(lax.div(group, N_CORE), N_YHI)
     y = N_YLO * y_hi + y_lo
     way = 1 - 2 * core
-    odd, pair = x % 2, x // 2
-
-    def device(dz, dx, dy):
-        x_to, y_to, z_to = (x + dx + N_X) % N_X, (y + dy + N_Y) % N_Y, (z + dz + N_Z) % N_Z
-        return (y_to % N_YLO) * N_Z + z_to, (x_to * N_YHI + y_to // N_YLO) * N_CORE + core
+    odd, pair = lax.rem(x, 2), lax.div(x, 2)
+
+    @functools.cache
+    def z_to(step, turn=0):
+        return lax.rem(z + way * step + N_Z + turn, N_Z)
+
+    @functools.cache
+    def x_to(step):
+        return lax.rem(x + way * step + N_X, N_X)
+
+    @functools.cache
+    def y_to(step):
+        to = lax.rem(y + way * step + N_Y, N_Y)
+        return lax.rem(to, N_YLO), lax.div(to, N_YLO)
+
+    @functools.cache
+    def slab_row(dz, dy):
+        return y_to(dy)[0] * N_Z + z_to(dz)
+
+    @functools.cache
+    def group_row(dx, dy):
+        return (x_to(dx) * N_YHI + y_to(dy)[1]) * N_CORE + core
 
     def to(k):
-        return device(*(way * d for d in OFFSETS[k]))
+        dz, dx, dy = OFFSETS[k]
+        return slab_row(dz, dy), group_row(dx, dy)
 
     def back(k):
-        return device(*(-way * d for d in OFFSETS[k]))
+        dz, dx, dy = (-d for d in OFFSETS[k])
+        return slab_row(dz, dy), group_row(dx, dy)
 
     def slab_of(k):
-        dz, dx, dy = (way * d for d in OFFSETS[k])
-        return ((y + dy + N_Y) % N_YLO) * N_Z + (z + dz + N_Z + FAR * ((x + dx + N_X) % 2)) % N_Z
+        dz, dx, dy = OFFSETS[k]
+        return y_to(dy)[0] * N_Z + lax.rem(z_to(dz) + FAR * lax.rem(x_to(dx), 2), N_Z)
+
+    @functools.cache
+    def y_hi_to(d):
+        return lax.rem(y_hi + d, N_YHI)
 
     def y_peer(d):
-        return device(0, 0, N_YLO * d)
-
-    x_peer = device(0, 2, 0)
+        return slab, (x * N_YHI + y_hi_to(d)) * N_CORE + core
+
+    x_peer = slab, (lax.rem(x + 2, N_X) * N_YHI + y_hi) * N_CORE + core
     sibling = (slab, group + way)
-    near, across, beyond = device(0, 1 - 2 * odd, 0), device(FAR, 1 - 2 * odd, 0), device(FAR, 0, 0)
+    far_slab = y_lo * N_Z + z_to(0, FAR)
+    near_group = ((x + 1 - 2 * odd) * N_YHI + y_hi) * N_CORE + core
+    near, across, beyond = (slab, near_group), (far_slab, near_group), (far_slab, group)
 
     def choose(a, b):
         return tuple(odd * v + (1 - odd) * u for u, v in zip(a, b))
@@ -148,6 +175,19 @@
     lines[0] = send_lines[0]
     tags[0] = send_tags[0]
 
+    k_loc = N_CORE * N_X * N_YHI * per
+    h_rows = k_loc // N_CORE
+    x_rows = h_rows // 2
+    ctf_sq4[...] = jnp.concatenate([ctf[...] * ctf[...]] * (128 // groups), axis=0).astype(BF16)
+    spread[...] = (iota((128, span), 0) == iota((128, span), 1) % cap).astype(F32).astype(BF16)
+    owner_row[...] = (iota((PER_BATCH * 8, span), 0) == 8 * (iota((PER_BATCH * 8, span), 1) // cap)).astype(F32)
+    tag_of[...] = (iota((128, span), 0) % groups + 1).astype(F32)
+    row_tile = (iota((h_rows, 128), 0) // 8) % (2 * per // 8)
+    own_lanes[...] = (iota((h_rows, 128), 1) // groups == row_tile).astype(F32)
+    at_lane = line_k - PER_BATCH * jnp.floor(line_k * (1.0 / PER_BATCH))
+    lane_hot[...] = (iota((span, rows), 0) == (at_lane * cap + rank).astype(jnp.int32)).astype(F32).astype(BF16)
+    hot_lines[...] = hot
+
     pl.semaphore_wait(barrier, len(partners) + odd)
     loads[3].wait()
 
@@ -173,8 +213,8 @@
         line_copy.start()
         return [tag_copy, line_copy]
 
-    for k in reversed(range(1, n)):
-        if OFFSETS[k][2] == 0:
+    for k in range(1, n):
+        if not (OFFSETS[k][2] or OFFSETS[k][1]):
             sends += send_slots(k)
 
     @pl.when(odd == 1)
@@ -187,24 +227,21 @@
     ag_y = [copy(mine, mine, s_agy.at[d - 1], r_agy.at[d - 1], y_peer(d)) for d in range(1, N_YHI)]
     for c in ag_y:
         c.start()
-    blocks = [ref_all.at[core, pair, (y_hi + N_YHI - d) % N_YHI] for d in range(N_YHI)]
+    blocks = [ref_all.at[core, pair, y_hi_to(N_YHI - d)] for d in range(N_YHI)]
     ag_x = [copy(p, p, s_agx.at[d], r_agx.at[d], x_peer) for d, p in enumerate(blocks)]
     ag_x[0].start()
 
-    for k in reversed(range(1, n)):
-        if OFFSETS[k][2]:
+    for k in range(1, n):
+        if OFFSETS[k][2] or OFFSETS[k][1]:
             sends += send_slots(k)
 
-    k_loc = N_CORE * N_X * N_YHI * per
-    ctf_sq = ctf[...] * ctf[...]
-    ctf_sq4 = jnp.concatenate([ctf_sq] * (128 // groups), axis=0).astype(BF16)
     p_rows = k_loc // 4
 
     def set_quad(c, p):
         reference = ref_all[c, p].reshape(p_rows, width)
         re, im = reference[:, :half].astype(F32), reference[:, half:].astype(F32)
         power = (re * re + im * im).astype(BF16)
-        hi, mid, lo = three(-0.5 * nt(power, ctf_sq4))
+        hi, mid, lo = three(-0.5 * nt(power, ctf_sq4[...]))
         lane = iota((p_rows, 128), 1)
         parts = jnp.where(lane < 2 * groups, mid.astype(F32), jnp.where(lane < 3 * groups, lo.astype(F32), 0.0))
         quad[c, p] = jnp.where(lane < groups, hi.astype(F32), parts).astype(BF16)
@@ -227,9 +264,6 @@
     sends += [ag] + ag_y + ag_x + ag_c
 
     scale = width**-0.5
-    spread = (iota((128, span), 0) == iota((128, span), 1) % cap).astype(F32).astype(BF16)
-    mine_8 = (iota((PER_BATCH * 8, span), 0) == 8 * (iota((PER_BATCH * 8, span), 1) // cap)).astype(F32)
-    tag_of = (iota((128, span), 0) % groups + 1).astype(F32)
     ev_sends = []
     for b in range(batches):
         for j in range(PER_BATCH):
@@ -240,8 +274,8 @@
         here = slice(b * span, (b + 1) * span)
         batch = lines[b * PER_BATCH : (b + 1) * PER_BATCH].reshape(span, width)
         tag8 = tags[b * PER_BATCH : (b + 1) * PER_BATCH].reshape(PER_BATCH * 8, 128).astype(BF16)
-        tag = jnp.sum(nn(tag8, spread) * mine_8, axis=0, keepdims=True)
-        pick = (tag_of == tag).astype(F32).astype(BF16)
+        tag = jnp.sum(nn(tag8, spread[...]) * owner_row[...], axis=0, keepdims=True)
+        pick = (tag_of[...] == tag).astype(F32).astype(BF16)
         chosen[:, here] = pick
         score = nt(ref_all[...].reshape(k_loc, width), batch) + nn(quad[...].reshape(k_loc, 128), pick)
         score *= scale
@@ -259,14 +293,10 @@
             else:
                 ev[0] = send_ev[0]
 
-    h_rows = k_loc // N_CORE
-    x_rows = h_rows // 2
-    own_lanes = iota((h_rows, 128), 1) // groups == (iota((h_rows, 128), 0) // 8) % (2 * per // 8)
-
     def sum_half(c):
         r = resp[pl.ds(pl.multiple_of(c * h_rows, h_rows), h_rows), :]
         acc[c] = nn(r, lines[...].reshape(n * cap, width))
-        count = jnp.where(own_lanes, nt(r, chosen[...]), 0.0)
+        count = nt(r, chosen[...]) * own_lanes[...]
         return jnp.sum(count.reshape(2, N_YHI, 2 * per // 8, 8, 128), axis=2)
 
     rcore_out[...] = sum_half(1 - core)
@@ -287,7 +317,7 @@
     core_sends[1].wait_recv()
 
     def rows_of(d, first=0):
-        at = first + ((y_hi + d) % N_YHI) * 2 * per
+        at = first + y_hi_to(d) * 2 * per
         return pl.ds(pl.multiple_of(at, 2 * per), 2 * per)
 
     for i, d in enumerate(turns):
@@ -308,7 +338,7 @@
         at = rows_of(d)
         y_out[d - 1] = (own_rows[at] + x_in[at].astype(F32)).astype(BF16)
         yc = copy(y_out.at[d - 1], y_in.at[d - 1], s_rsy.at[d - 1], r_rsy.at[d - 1], y_peer(d))
-        rcy = copy(ry_out.at[(y_hi + d) % N_YHI], ry_in.at[d - 1], s_rcy.at[d - 1], r_rcy.at[d - 1], y_peer(d))
+        rcy = copy(ry_out.at[y_hi_to(d)], ry_in.at[d - 1], s_rcy.at[d - 1], r_rcy.at[d - 1], y_peer(d))
         rcy.start()
         yc.start()
         y_sends += [rcy, yc]
@@ -317,11 +347,9 @@
 
     for c in ev_sends:
         c.wait_recv()
-    at_lane = line_k - PER_BATCH * jnp.floor(line_k * (1.0 / PER_BATCH))
-    lane_hot = (iota((span, rows), 0) == (at_lane * cap + rank).astype(jnp.int32)).astype(F32).astype(BF16)
     e_hi, e_mid, e_lo = three(ev[:, 0, :])
-    by_target = nn(e_hi, lane_hot) + nn(e_mid, lane_hot) + nn(e_lo, lane_hot)
-    line_ev[...] = jnp.sum(hot * by_target, axis=0, keepdims=True)
+    by_target = nn(e_hi, lane_hot[...]) + nn(e_mid, lane_hot[...]) + nn(e_lo, lane_hot[...])
+    line_ev[...] = jnp.sum(hot_lines[...] * by_target, axis=0, keepdims=True)
 
     at = rows_of(0)
     part = own_rows[at] + x_in[at].astype(F32)
@@ -364,7 +392,7 @@
     cnt = jnp.concatenate([tile] * (per // 8), axis=0)
     cnt = jnp.where(iota((per, 128), 1) // groups == iota((per, 128), 0) // 8 + odd * (per // 8), cnt, 0.0)
     c_hi, c_mid, c_lo = three(cnt)
-    den = nn(c_hi, ctf_sq4) + nn(c_mid, ctf_sq4) + nn(c_lo, ctf_sq4) + 1.0
+    den = nn(c_hi, ctf_sq4[...]) + nn(c_mid, ctf_sq4[...]) + nn(c_lo, ctf_sq4[...]) + 1.0
     out[:, :half] = final[:, :half] / den
     out[:, half:] = final[:, half:] / den
 
@@ -400,6 +428,8 @@
         vm((N_YHI - 1, 2 * per, width), BF16), vm((N_YHI - 1, 2 * per, width), BF16),
         vm((N_YHI, 8, 128), F32), vm((N_YHI - 1, 8, 128), F32),
         vm((2, per, width), BF16), vm((2, per, width), BF16), vm((8, 128), F32), vm((2, 8, 128), F32),
+        vm((128, width // 2), BF16), vm((128, PER_BATCH * cap), BF16), vm((PER_BATCH * 8, PER_BATCH * cap), F32),
+        vm((128, PER_BATCH * cap), F32), vm((h_rows, 128), F32), vm((PER_BATCH * cap, rows), BF16), vm((n, rows), F32),
         dma((5,)),
         *[dma((n,))] * 6,
         *[dma((2,))] * 2, *[dma((N_YHI - 1,))] * 2, *[dma((N_YHI,))] * 2, *[dma((2,))] * 2,

time: 60.9 us -> 59.2 us (0.972)
  the two profiles are of different devices: /device:TPU:8 before, /device:TPU:1 now
where the time goes in v6:
time: 59.2 us; the launch traced here: 58.2 us
  Pallas kernels  55.6 us (94%)
  local copies, waits for them, and re-layouts  1.99 us (3%)
  between operations  0.65 us (1%)
    pallas_call x1, Pallas kernels, on_device(): pl.pallas_call(kernel, out_shape=(jax.ShapeDtypeStruct((per, width), F32)...  55.6 us
    unnamed x4, local copies, waits for them, and re-layouts  1.99 us

profile of v6, /device:TPU:1, one launch (start us, length us, event | category | flops | bytes accessed | tf_op | source)
XLA Modules:
  0.0 58.2 jit_solution(11780381654783252617)
XLA Ops:
  0.6 55.6 %shard_map.68 = (f32[16,768]{1,0:T(8,128)}, f32[1,256]{1,0:T(1,128)}) custom-call(bf16[256,768]{1,0:T(8,128)(2,1)} %img_hbm.1, bf16[16,768]{1,0:T(8,128)(2,1)} %refs_hbm.1, f32[32,384]{1,0:T(8,128)} %ctf_hbm.1, s32[1,256]{1,0:T(1,128)} %bitcast.3, s32[1,256]{1,0:T(1,128)} %bitcast.4), custom_call_target="tpu_custom_call" | custom-call | tf_op jit(solution)/shard_map/pallas_call | solution.py:439
  56.2 0.0 copy-start
  56.2 1.4 %copy.9 = f32[16,768]{1,0:T(8,128)} copy(f32[16,768]{1,0:T(8,128)} %get-tuple-element.8) | data formatting | bytes 98304
  57.7 0.0 copy-done
  57.7 0.6 copy.10
Async XLA Ops:
  56.2 1.4 %copy-start = (f32[1,256]{1,0:T(1,128)S(1)}, f32[1,256]{1,0:T(1,128)}, u32[]{:S(2)}) copy-start(f32[1,256]{1,0:T(1,128)} %get-tuple-element.5) | copy-start | bytes 3076

commit v7 on v6

--- a/solution.py
+++ b/solution.py
@@ -332,16 +332,28 @@
     rc.wait_recv()
     own_cnt = rx_out[pair] + rx_in[...]
     ry_out[...] = own_cnt
-    y_sends = []
-    for i, d in enumerate(turns[:-1]):
-        x_sends[i].wait_recv()
-        at = rows_of(d)
-        y_out[d - 1] = (own_rows[at] + x_in[at].astype(F32)).astype(BF16)
-        yc = copy(y_out.at[d - 1], y_in.at[d - 1], s_rsy.at[d - 1], r_rsy.at[d - 1], y_peer(d))
-        rcy = copy(ry_out.at[y_hi_to(d)], ry_in.at[d - 1], s_rcy.at[d - 1], r_rcy.at[d - 1], y_peer(d))
-        rcy.start()
-        yc.start()
-        y_sends += [rcy, yc]
+    halves = 1 - odd, odd
+
+    def half_of(d, h):
+        return pl.ds(pl.multiple_of(y_hi_to(d) * 2 * per + halves[h] * per, per), per)
+
+    count_sends = []
+    for d in turns[:-1]:
+        count_sends.append(
+            copy(ry_out.at[y_hi_to(d)], ry_in.at[d - 1], s_rcy.at[d - 1], r_rcy.at[d - 1], y_peer(d))
+        )
+        count_sends[-1].start()
+    y_sends = [[], []]
+    for h in range(2):
+        for i, d in enumerate(turns[:-1]):
+            if h == 0:
+                x_sends[i].wait_recv()
+            at = half_of(d, h)
+            y_out[h, d - 1] = (own_rows[at] + x_in[at].astype(F32)).astype(BF16)
+            y_sends[h].append(
+                copy(y_out.at[h, d - 1], y_in.at[h, d - 1], s_rsy.at[h, d - 1], r_rsy.at[h, d - 1], y_peer(d))
+            )
+            y_sends[h][-1].start()
     x_sends[-1].wait_recv()
     x_sends.append(rc)
 
@@ -351,16 +363,20 @@
     by_target = nn(e_hi, lane_hot[...]) + nn(e_mid, lane_hot[...]) + nn(e_lo, lane_hot[...])
     line_ev[...] = jnp.sum(hot_lines[...] * by_target, axis=0, keepdims=True)
 
-    at = rows_of(0)
-    part = own_rows[at] + x_in[at].astype(F32)
-    for c in y_sends:
+    count = ry_out[y_hi]
+    for c in count_sends:
         c.wait_recv()
-    count = ry_out[y_hi]
     for d in range(1, N_YHI):
-        part += y_in[d - 1].astype(F32)
         count += ry_in[d - 1]
-    fin_out[...] = part.reshape(2, per, width).astype(BF16)
     rfin_out[...] = count
+
+    def finish(h):
+        part = own_rows[half_of(0, h)] + x_in[half_of(0, h)].astype(F32)
+        for c in y_sends[h]:
+            c.wait_recv()
+        for d in range(1, N_YHI):
+            part += y_in[h, d - 1].astype(F32)
+        fin_out[halves[h]] = part.astype(BF16)
 
     def fins(src, dst, i, dev):
         return (
@@ -370,8 +386,10 @@
 
     fin = fins(1 - odd, odd, 0, choose(near, across))
     fin_2 = fins(1, 1, 1, beyond)
+    finish(0)
     for c in fin:
         c.start()
+    finish(1)
 
     @pl.when(odd == 1)
     def _():
@@ -401,7 +419,7 @@
         for c in fin_2:
             c.wait_send()
 
-    for c in sends + ev_sends + core_sends + x_sends + y_sends + list(fin):
+    for c in sends + ev_sends + core_sends + x_sends + count_sends + y_sends[0] + y_sends[1] + list(fin):
         c.wait_send()
 
 
@@ -425,7 +443,7 @@
         vm((h_rows, width), F32), vm((2, N_YHI, 8, 128), F32), vm((2, N_YHI, 8, 128), F32),
         vm((x_rows, width), BF16), vm((x_rows, width), BF16), vm((2, N_YHI, 8, 128), F32), vm((N_YHI, 8, 128), F32),
         vm((x_rows, width), F32),
-        vm((N_YHI - 1, 2 * per, width), BF16), vm((N_YHI - 1, 2 * per, width), BF16),
+        vm((2, N_YHI - 1, per, width), BF16), vm((2, N_YHI - 1, per, width), BF16),
         vm((N_YHI, 8, 128), F32), vm((N_YHI - 1, 8, 128), F32),
         vm((2, per, width), BF16), vm((2, per, width), BF16), vm((8, 128), F32), vm((2, 8, 128), F32),
         vm((128, width // 2), BF16), vm((128, PER_BATCH * cap), BF16), vm((PER_BATCH * 8, PER_BATCH * cap), F32),
@@ -433,7 +451,7 @@
         dma((5,)),
         *[dma((n,))] * 6,
         *[dma((2,))] * 2, *[dma((N_YHI - 1,))] * 2, *[dma((N_YHI,))] * 2, *[dma((2,))] * 2,
-        *[dma((2,))] * 2, *[dma] * 2, *[dma((N_YHI,))] * 2, *[dma] * 2, *[dma((N_YHI - 1,))] * 4,
+        *[dma((2,))] * 2, *[dma] * 2, *[dma((N_YHI,))] * 2, *[dma] * 2, *[dma((2, N_YHI - 1))] * 2, *[dma((N_YHI - 1,))] * 2,
         *[dma((2,))] * 4,
     ]
     new, ev = pl.pallas_call(

time: 59.2 us -> 58.7 us (level)
  no operation moved by 1% of the time
where the time goes in v7:
time: 58.7 us; the launch traced here: 57.8 us
  Pallas kernels  55.2 us (94%)
  local copies, waits for them, and re-layouts  1.99 us (3%)
  between operations  0.65 us (1%)
    pallas_call x1, Pallas kernels, on_device(): pl.pallas_call(kernel, out_shape=(jax.ShapeDtypeStruct((per, width), F32)...  55.2 us
    unnamed x4, local copies, waits for them, and re-layouts  1.99 us

profile of v7, /device:TPU:1, one launch (start us, length us, event | category | flops | bytes accessed | tf_op | source)
XLA Modules:
  0.0 57.8 jit_solution(251626942650721059)
XLA Ops:
  0.6 55.2 %shard_map.68 = (f32[16,768]{1,0:T(8,128)}, f32[1,256]{1,0:T(1,128)}) custom-call(bf16[256,768]{1,0:T(8,128)(2,1)} %img_hbm.1, bf16[16,768]{1,0:T(8,128)(2,1)} %refs_hbm.1, f32[32,384]{1,0:T(8,128)} %ctf_hbm.1, s32[1,256]{1,0:T(1,128)} %bitcast.3, s32[1,256]{1,0:T(1,128)} %bitcast.4), custom_call_target="tpu_custom_call" | custom-call | tf_op jit(solution)/shard_map/pallas_call | solution.py:457
  55.8 0.0 copy-start
  55.8 1.4 %copy.9 = f32[16,768]{1,0:T(8,128)} copy(f32[16,768]{1,0:T(8,128)} %get-tuple-element.8) | data formatting | bytes 98304
  57.2 0.0 copy-done
  57.2 0.6 copy.10
Async XLA Ops:
  55.8 1.4 %copy-start = (f32[1,256]{1,0:T(1,128)S(1)}, f32[1,256]{1,0:T(1,128)}, u32[]{:S(2)}) copy-start(f32[1,256]{1,0:T(1,128)} %get-tuple-element.5) | copy-start | bytes 3076

commit v8 on v7

--- a/solution.py
+++ b/solution.py
@@ -158,7 +158,7 @@
     rank_hot = (iota((128, rows), 0) == rank.astype(jnp.int32)).astype(F32).astype(BF16)
     tag_slots = nt((hot * tag_row).astype(BF16), rank_hot)
     for k in range(n):
-        send_tags[k] = jnp.broadcast_to(tag_slots[k : k + 1, :], (8, 128))
+        send_tags[k] = tag_slots[k : k + 1, :]
 
     pick = (iota((groups, rows), 0) == ids[...]).astype(F32).astype(BF16)
     ctf_hi, ctf_mid, ctf_lo = three(ctf[...])
@@ -180,7 +180,7 @@
     x_rows = h_rows // 2
     ctf_sq4[...] = jnp.concatenate([ctf[...] * ctf[...]] * (128 // groups), axis=0).astype(BF16)
     spread[...] = (iota((128, span), 0) == iota((128, span), 1) % cap).astype(F32).astype(BF16)
-    owner_row[...] = (iota((PER_BATCH * 8, span), 0) == 8 * (iota((PER_BATCH * 8, span), 1) // cap)).astype(F32)
+    owner_row[...] = (iota((PER_BATCH, span), 0) == iota((PER_BATCH, span), 1) // cap).astype(F32)
     tag_of[...] = (iota((128, span), 0) % groups + 1).astype(F32)
     row_tile = (iota((h_rows, 128), 0) // 8) % (2 * per // 8)
     own_lanes[...] = (iota((h_rows, 128), 1) // groups == row_tile).astype(F32)
@@ -273,7 +273,7 @@
                 copy(send_lines.at[k], lines.at[k], s_line.at[k], r_line.at[k], to(k)).wait_recv()
         here = slice(b * span, (b + 1) * span)
         batch = lines[b * PER_BATCH : (b + 1) * PER_BATCH].reshape(span, width)
-        tag8 = tags[b * PER_BATCH : (b + 1) * PER_BATCH].reshape(PER_BATCH * 8, 128).astype(BF16)
+        tag8 = tags[b * PER_BATCH : (b + 1) * PER_BATCH, 0, :].astype(BF16)
         tag = jnp.sum(nn(tag8, spread[...]) * owner_row[...], axis=0, keepdims=True)
         pick = (tag_of[...] == tag).astype(F32).astype(BF16)
         chosen[:, here] = pick
@@ -436,7 +436,7 @@
         vm((rows, width), BF16), vm((per, width), BF16), vm(ctf_table.shape, F32),
         vm((1, rows), jnp.int32), vm((1, rows), jnp.int32),
         vm((rows, width), BF16), vm((n, cap, width), BF16), vm((n, cap, width), BF16),
-        vm((n, 8, 128), F32), vm((n, 8, 128), F32),
+        vm((n, 1, 128), F32), vm((n, 1, 128), F32),
         vm((n // PER_BATCH, 1, PER_BATCH * cap), F32), vm((n, 1, PER_BATCH * cap), F32),
         vm((N_CORE, 2, N_YHI, 2, per, width), BF16), vm((N_CORE * h_rows, n * cap), BF16), vm((128, n * cap), BF16),
         vm((N_CORE, 2, x_rows, 128), BF16), vm((N_CORE, h_rows, width), F32), vm((2, N_YHI, 8, 128), F32),
@@ -446,7 +446,7 @@
         vm((2, N_YHI - 1, per, width), BF16), vm((2, N_YHI - 1, per, width), BF16),
         vm((N_YHI, 8, 128), F32), vm((N_YHI - 1, 8, 128), F32),
         vm((2, per, width), BF16), vm((2, per, width), BF16), vm((8, 128), F32), vm((2, 8, 128), F32),
-        vm((128, width // 2), BF16), vm((128, PER_BATCH * cap), BF16), vm((PER_BATCH * 8, PER_BATCH * cap), F32),
+        vm((128, width // 2), BF16), vm((128, PER_BATCH * cap), BF16), vm((PER_BATCH, PER_BATCH * cap), F32),
         vm((128, PER_BATCH * cap), F32), vm((h_rows, 128), F32), vm((PER_BATCH * cap, rows), BF16), vm((n, rows), F32),
         dma((5,)),
         *[dma((n,))] * 6,

time: 58.7 us -> 58.7 us (level)
  the two profiles are of different devices: /device:TPU:1 before, /device:TPU:8 now
where the time goes in v8:
time: 58.7 us; the launch traced here: 58.5 us
  Pallas kernels  55.9 us (95%)
  local copies, waits for them, and re-layouts  1.99 us (3%)
  between operations  0.65 us (1%)
    pallas_call x1, Pallas kernels, on_device(): pl.pallas_call(kernel, out_shape=(jax.ShapeDtypeStruct((per, width), F32)...  55.9 us
    unnamed x4, local copies, waits for them, and re-layouts  1.99 us

profile of v8, /device:TPU:8, one launch (start us, length us, event | category | flops | bytes accessed | tf_op | source)
XLA Modules:
  0.0 58.5 jit_solution(2139381482868509241)
XLA Ops:
  0.6 55.9 %shard_map.68 = (f32[16,768]{1,0:T(8,128)}, f32[1,256]{1,0:T(1,128)}) custom-call(bf16[256,768]{1,0:T(8,128)(2,1)} %img_hbm.1, bf16[16,768]{1,0:T(8,128)(2,1)} %refs_hbm.1, f32[32,384]{1,0:T(8,128)} %ctf_hbm.1, s32[1,256]{1,0:T(1,128)} %bitcast.3, s32[1,256]{1,0:T(1,128)} %bitcast.4), custom_call_target="tpu_custom_call" | custom-call | tf_op jit(solution)/shard_map/pallas_call | solution.py:457
  56.5 0.0 copy-start
  56.5 1.4 %copy.9 = f32[16,768]{1,0:T(8,128)} copy(f32[16,768]{1,0:T(8,128)} %get-tuple-element.8) | data formatting | bytes 98304
  58.0 0.0 copy-done
  58.0 0.6 copy.10
Async XLA Ops:
  56.5 1.4 %copy-start = (f32[1,256]{1,0:T(1,128)S(1)}, f32[1,256]{1,0:T(1,128)}, u32[]{:S(2)}) copy-start(f32[1,256]{1,0:T(1,128)} %get-tuple-element.5) | copy-start | bytes 3076
